TPU v7x, 128 devices: a whole 4x4x4 slice. The times are simulated.
128 devices in a mesh: ctx: 16 (over y, z), vocab: 8 (over x, core).
Axes of the slice: x: 4, y: 4, z: 4, core: 2. Of those that a mesh axis runs over, the one named last changes fastest.
Arguments:
- hidden_policy: bfloat16 [2, 512, 5120], P(None, 'ctx', 'vocab'), may hold values from -360 to 360, as said below
- hidden_ref: bfloat16 [2, 512, 5120], P(None, 'ctx', 'vocab'), may hold values from -360 to 360, as said below
- head_policy: bfloat16 [5120, 147456], P(None, ('ctx', 'vocab')), may hold values from -0.078125 to 0.078125
- head_ref: bfloat16 [5120, 147456], P(None, ('ctx', 'vocab')), may hold values from -0.078125 to 0.078125
- token_ids: int32 [2, 512], P(None, 'ctx'), may hold values from 0 to 147455
- response_mask: int32 [2, 512], P(None, 'ctx'), may hold values 0 or 1
- done_flags: int32 [2, 512], P(None, 'ctx'), may hold values 0 or 1
- scores: float32 [2, 512], P(None, 'ctx'), may hold values from -6 to 6
- values: float32 [2, 512], P(None, 'ctx'), may hold values from -6 to 6
Outputs:
- rewards: float32 [2, 512], P(None, 'ctx')
- advantages: float32 [2, 512], P(None, 'ctx')
- returns: float32 [2, 512], P(None, 'ctx')
- logprobs: float32 [2, 512], P(None, 'ctx')
Inputs may be any that keep to these rules, and one draw needn't show every extreme that they name: `hidden_policy`: each token's hidden state has a scale of its own. `hidden_ref`: each token's hidden state has a scale of its own.
All inputs are finite; a program needn't handle non-finite values. No bound on the sum of `response_mask` or of `done_flags` on one device may be relied on, other than what follows from the above.
Results may differ from a plain program's by a relative error of at most 0.0003.
Values may be sent and summed in bfloat16 or wider, within the bound.
No kernel may reach another device: no remote copies, remote signals or barrier semaphores. Data moves between devices by JAX's collectives and lax.ppermute only.
A program may use at most 128 MiB of HBM per device.

v0:
```python
import jax
import jax.numpy as jnp
from jax import lax
from jax.sharding import PartitionSpec as P


def merged_2(x, axis, combine):
    everything = jax.tree.map(lambda part: lax.all_gather(part, axis), x)
    leading = jax.tree.map(lambda part: part[0], everything)

    def turn(k, so_far):
        return combine(so_far, jax.tree.map(lambda part: part[k], everything))

    return lax.fori_loop(1, lax.axis_size(axis), turn, leading)


def from_behind(value, axis, steps):
    count = lax.axis_size(axis)
    leading, last = (max(0, -steps), min(count, count - steps))
    return lax.ppermute(value, axis, [(source, source + steps) for source in range(leading, last)])


def combine_stats(first, second):
    m_a, s_a, t_a, n_a, q_a, c_a = first
    m_b, s_b, t_b, n_b, q_b, c_b = second
    top_p = jnp.maximum(m_a, m_b)
    w_a = jnp.exp(m_a - top_p)
    w_b = jnp.exp(m_b - top_p)
    top_q = jnp.maximum(n_a, n_b)
    return (
        top_p,
        s_a * w_a + s_b * w_b,
        t_a * w_a + t_b * w_b,
        top_q,
        q_a * jnp.exp(n_a - top_q) + q_b * jnp.exp(n_b - top_q),
        c_a + c_b,
    )


def body(
    hidden_policy,
    hidden_ref,
    head_policy,
    head_ref,
    token_ids,
    response_mask,
    done_flags,
    scores,
    values,
):
    full_p, full_q = (
        lax.all_gather(hidden_policy, "vocab", axis=2, tiled=True),
        lax.all_gather(hidden_ref, "vocab", axis=2, tiled=True),
    )
    ids_all = lax.all_gather(token_ids, "ctx", axis=1, tiled=True)
    n_ctx = lax.axis_size("ctx")
    n_vocab = lax.axis_size("vocab")
    width = head_policy.shape[1]
    seqs = token_ids.shape[0]
    tok_dev = token_ids.shape[1]
    col_start = (lax.axis_index("ctx") * n_vocab + lax.axis_index("vocab")) * width
    piece_p, piece_q = lax.all_gather((full_p, full_q), "ctx", axis=1, tiled=True)
    logits_p = jnp.einsum("btd,dv->btv", piece_p, head_policy, preferred_element_type=jnp.float32)
    logits_q = jnp.einsum("btd,dv->btv", piece_q, head_ref, preferred_element_type=jnp.float32)
    top_p = jnp.max(logits_p, axis=-1)
    expo = jnp.exp(logits_p - top_p[..., None])
    sum_p = jnp.sum(expo, axis=-1)
    cross = jnp.sum(expo * (logits_p - logits_q), axis=-1)
    top_q = jnp.max(logits_q, axis=-1)
    sum_q = jnp.sum(jnp.exp(logits_q - top_q[..., None]), axis=-1)
    local_ids = ids_all - col_start
    column = lax.broadcasted_iota(jnp.int32, logits_p.shape, 2)
    chosen = jnp.sum(jnp.where(column == local_ids[..., None], logits_p, 0.0), axis=-1)
    stats = (top_p, sum_p, cross, top_q, sum_q, chosen)
    merged = merged_2(stats, ("ctx", "vocab"), combine_stats)
    offset = lax.axis_index("ctx") * tok_dev
    own = tuple((lax.dynamic_slice_in_dim(item, offset, tok_dev, 1) for item in merged))
    top_p, sum_p, cross, top_q, sum_q, chosen = own
    lz_p = top_p + jnp.log(sum_p)
    lz_q = top_q + jnp.log(sum_q)
    kl_val = cross / sum_p - lz_p + lz_q
    logprobs = chosen - lz_p
    mask = response_mask.astype(jnp.float32)
    done = done_flags.astype(jnp.float32)
    rewards = -0.05 * mask * kl_val + done * scores
    following = from_behind(values[:, :1], "ctx", -1)
    next_value = jnp.concatenate([values[:, 1:], following], axis=1)
    delta = rewards + (1.0 - done) * next_value - values
    coef = 0.998 * (1.0 - done)

    def step(carry, item):
        acc, prod = carry
        cval, dval = item
        acc = dval + cval * acc
        prod = cval * prod
        return ((acc, prod), (acc, prod))

    start_carry = (jnp.zeros((seqs,), jnp.float32), jnp.ones((seqs,), jnp.float32))
    _, (local_gae, decay) = lax.scan(step, start_carry, (coef.T, delta.T), reverse=True)
    local_gae = local_gae.T
    decay = decay.T
    head_gae = local_gae[:, 0]
    head_decay = decay[:, 0]

    def relay(index, incoming):
        return from_behind(head_gae + head_decay * incoming, "ctx", -1)

    incoming = lax.fori_loop(0, n_ctx - 1, relay, jnp.zeros((seqs,), jnp.float32))
    gae = local_gae + decay * incoming[:, None]
    return (rewards, mask * gae, mask * (gae + values), logprobs)


def solution(mesh):
    placed = (
        P(None, "ctx", "vocab"),
        P(None, "ctx", "vocab"),
        P(None, ("ctx", "vocab")),
        P(None, ("ctx", "vocab")),
        P(None, "ctx"),
        P(None, "ctx"),
        P(None, "ctx"),
        P(None, "ctx"),
        P(None, "ctx"),
    )
    return jax.shard_map(
        body,
        mesh=mesh,
        in_specs=placed,
        out_specs=(P(None, "ctx"), P(None, "ctx"), P(None, "ctx"), P(None, "ctx")),
        check_vma=False,
    )
```

profile of v0, /device:TPU:0, one launch (start us, length us, event | category | flops | bytes accessed | tf_op | source)
XLA Modules:
  0.0 544.2 jit_solution(12757296034619252240)
XLA Ops:
  7.2 15.1 %all_gather.51 = bf16[2,32,5120]{2,1,0:T(8,128)(2,1)} all-gather(bf16[2,32,640]{2,1,0:T(8,128)(2,1)} %param.15), channel_id=1, replica_groups=mesh['ctx'=16,'vocab'=8] {'vocab'}, dimensions={2}, use_global_device_ids=true | all-gather | bytes 737280 | tf_op jit(solution)/shard_map/all_gather | solution.py:52
  22.4 14.6 %all_gather.57 = bf16[2,32,5120]{2,1,0:T(8,128)(2,1)} all-gather(bf16[2,32,640]{2,1,0:T(8,128)(2,1)} %param.16), channel_id=1, replica_groups=mesh['ctx'=16,'vocab'=8] {'vocab'}, dimensions={2}, use_global_device_ids=true | all-gather | bytes 737280 | tf_op jit(solution)/shard_map/all_gather | solution.py:53
  37.0 1.3 collective-permute-start.1
  39.1 28.1 %all-gather.11 = s32[16,32,2]{1,2,0:T(2,128)S(1)} all-gather(s32[1,32,2]{1,2,0:T(2,128)} %bitcast.118), channel_id=1, replica_groups=mesh['ctx'=16,'vocab'=8] {'ctx'}, dimensions={0}, use_global_device_ids=true | all-gather | bytes 4352 | tf_op jit(solution)/shard_map/all_gather | solution.py:55
  67.3 37.5 %all-gather.16.cloned.1.call-done = bf16[2,512,5120]{2,1,0:T(8,128)(2,1)} async-done(((bf16[2,32,5120]{2,1,0:T(8,128)(2,1)}), bf16[2,512,5120]{2,1,0:T(8,128)(2,1)}) %all-gather.16.cloned.1.call-update) | async-done | bytes 10485776 | tf_op jit(solution)/shard_map/all_gather | solution.py:62
  104.8 19.3 %fusion.25 = (f32[2,512]{1,0:T(2,128)S(1)}, f32[2,512,1152]{2,1,0:T(8,128)}) fusion(bf16[2,512,5120]{2,1,0:T(8,128)(2,1)} %all-gather.16.cloned.1.call-done, bf16[5120,1152]{1,0:T(8,128)(2,1)} %param.17), kind=kOutput, calls=%fused_computation.63 | convolution fusion | flops 12080774144 | bytes 27004928 | tf_op jit(solution)/shard_map/btd,dv->btv/dot_general | solution.py:63
  124.2 62.9 %all-gather.18.cloned.1.call-done = bf16[2,512,5120]{2,1,0:T(8,128)(2,1)} async-done(((bf16[2,32,5120]{2,1,0:T(8,128)(2,1)}), bf16[2,512,5120]{2,1,0:T(8,128)(2,1)}) %all-gather.18.cloned.1.call-update) | async-done | bytes 10485776 | tf_op jit(solution)/shard_map/all_gather | solution.py:62
  187.0 17.3 %fusion.26 = (f32[2,512]{1,0:T(2,128)S(1)}, f32[2,512,1152]{2,1,0:T(8,128)S(1)}) fusion(bf16[2,512,5120]{2,1,0:T(8,128)(2,1)} %all-gather.18.cloned.1.call-done, bf16[5120,1152]{1,0:T(8,128)(2,1)} %param.18), kind=kOutput, calls=%fused_computation.64 | convolution fusion | flops 12080774144 | bytes 27004928 | tf_op jit(solution)/shard_map/btd,dv->btv/dot_general | solution.py:64
  204.4 2.7 multiply_reduce_fusion
  207.2 36.1 %all-gather.12 = f32[128,2,512]{2,1,0:T(2,128)S(1)} all-gather(f32[1,2,512]{2,1,0:T(2,128)S(1)} %bitcast.113), channel_id=7, replica_groups=mesh['ctx'=16,'vocab'=8] {'ctx','vocab'}, dimensions={0}, use_global_device_ids=true | all-gather | bytes 528384 | tf_op jit(solution)/shard_map/all_gather | solution.py:8
  243.2 34.0 %all-gather.10 = f32[128,2,512]{2,1,0:T(2,128)S(1)} all-gather(f32[1,2,512]{2,1,0:T(2,128)S(1)} %bitcast.112), channel_id=6, replica_groups=mesh['ctx'=16,'vocab'=8] {'ctx','vocab'}, dimensions={0}, use_global_device_ids=true | all-gather | bytes 528384 | tf_op jit(solution)/shard_map/all_gather | solution.py:8
  277.2 33.8 %all-gather.8 = f32[128,2,512]{2,1,0:T(2,128)S(1)} all-gather(f32[1,2,512]{2,1,0:T(2,128)S(1)} %bitcast.111), channel_id=4, replica_groups=mesh['ctx'=16,'vocab'=8] {'ctx','vocab'}, dimensions={0}, use_global_device_ids=true | all-gather | bytes 528384 | tf_op jit(solution)/shard_map/all_gather | solution.py:8
  311.1 33.8 %all-gather.7 = f32[128,2,512]{2,1,0:T(2,128)S(1)} all-gather(f32[1,2,512]{2,1,0:T(2,128)S(1)} %bitcast.110), channel_id=3, replica_groups=mesh['ctx'=16,'vocab'=8] {'ctx','vocab'}, dimensions={0}, use_global_device_ids=true | all-gather | bytes 528384 | tf_op jit(solution)/shard_map/all_gather | solution.py:8
  344.9 33.8 %all-gather.9 = f32[128,2,512]{2,1,0:T(2,128)S(1)} all-gather(f32[1,2,512]{2,1,0:T(2,128)S(1)} %bitcast.109), channel_id=5, replica_groups=mesh['ctx'=16,'vocab'=8] {'ctx','vocab'}, dimensions={0}, use_global_device_ids=true | all-gather | bytes 528384 | tf_op jit(solution)/shard_map/all_gather | solution.py:8
  378.7 33.8 %all-gather.6 = f32[128,2,512]{2,1,0:T(2,128)S(1)} all-gather(f32[1,2,512]{2,1,0:T(2,128)S(1)} %bitcast.108), channel_id=2, replica_groups=mesh['ctx'=16,'vocab'=8] {'ctx','vocab'}, dimensions={0}, use_global_device_ids=true | all-gather | bytes 528384 | tf_op jit(solution)/shard_map/all_gather | solution.py:8
  412.5 16.3 %while.56 = (s32[]{:T(128)}, f32[2,512]{1,0:T(2,128)S(1)}, f32[2,512]{1,0:T(2,128)S(1)}, f32[2,512]{1,0:T(2,128)S(1)}, f32[2,512]{1,0:T(2,128)S(1)}, /*index=5*/...) while((s32[]{:T(128)}, f32[2,512]{1,0:T(2,128)S(1)}, ...), condition=%wide.region_7.8_spmd, body=%wide.region_6.7_spmd.sunk | while | flops 18437 | bytes 94411 | solution.py:14
  429.7 3.7 while.58
  433.7 103.0 %while.57 = (s32[]{:T(128)}, f32[2]{0:T(128)S(1)}, f32[2]{0:T(128)S(1)}, f32[2]{0:T(128)S(1)}, s32[]{:T(128)}) while((s32[]{:T(128)}, f32[2]{0:T(128)S(1)}, f32[2]{0:T(128)S(1)}, f32[2]{0:T(128)S(1)}, s32[]{:T(128)}) %tuple.116), condition=%wide.region_11.12_spmd, body=%wide.region_10.11_spmd.sunk | while | flops 6 | bytes 165 | solution.py:108
  433.7 1.3 collective-permute-start
  435.0 4.1 collective-permute-done
  439.1 1.3 collective-permute-start
  440.4 4.1 collective-permute-done
  444.6 1.3 collective-permute-start
  445.9 4.1 collective-permute-done
  450.0 1.3 collective-permute-start
  451.3 4.1 collective-permute-done
  455.4 1.3 collective-permute-start
  456.7 4.6 collective-permute-done
  461.3 1.3 collective-permute-start
  462.6 6.2 %collective-permute-done = f32[2]{0:T(128)S(1)} collective-permute-done((f32[2]{0:T(128)S(1)}, f32[2]{0:T(128)S(1)}, u32[]{:S(2)}, u32[]{:S(2)}) %collective-permute-start) | collective-permute-done | bytes 40 | tf_op jit(solution)/shard_map/while/body/eval_jaxpr/ppermute | solution.py:20
  468.9 1.3 collective-permute-start
  470.2 6.2 %collective-permute-done = f32[2]{0:T(128)S(1)} collective-permute-done((f32[2]{0:T(128)S(1)}, f32[2]{0:T(128)S(1)}, u32[]{:S(2)}, u32[]{:S(2)}) %collective-permute-start) | collective-permute-done | bytes 40 | tf_op jit(solution)/shard_map/while/body/eval_jaxpr/ppermute | solution.py:20
  476.4 1.3 collective-permute-start
  477.7 6.2 %collective-permute-done = f32[2]{0:T(128)S(1)} collective-permute-done((f32[2]{0:T(128)S(1)}, f32[2]{0:T(128)S(1)}, u32[]{:S(2)}, u32[]{:S(2)}) %collective-permute-start) | collective-permute-done | bytes 40 | tf_op jit(solution)/shard_map/while/body/eval_jaxpr/ppermute | solution.py:20
  483.9 1.3 collective-permute-start
  485.2 6.2 %collective-permute-done = f32[2]{0:T(128)S(1)} collective-permute-done((f32[2]{0:T(128)S(1)}, f32[2]{0:T(128)S(1)}, u32[]{:S(2)}, u32[]{:S(2)}) %collective-permute-start) | collective-permute-done | bytes 40 | tf_op jit(solution)/shard_map/while/body/eval_jaxpr/ppermute | solution.py:20
  491.5 1.3 collective-permute-start
  492.8 6.2 %collective-permute-done = f32[2]{0:T(128)S(1)} collective-permute-done((f32[2]{0:T(128)S(1)}, f32[2]{0:T(128)S(1)}, u32[]{:S(2)}, u32[]{:S(2)}) %collective-permute-start) | collective-permute-done | bytes 40 | tf_op jit(solution)/shard_map/while/body/eval_jaxpr/ppermute | solution.py:20
  499.0 1.3 collective-permute-start
  500.3 6.2 %collective-permute-done = f32[2]{0:T(128)S(1)} collective-permute-done((f32[2]{0:T(128)S(1)}, f32[2]{0:T(128)S(1)}, u32[]{:S(2)}, u32[]{:S(2)}) %collective-permute-start) | collective-permute-done | bytes 40 | tf_op jit(solution)/shard_map/while/body/eval_jaxpr/ppermute | solution.py:20
  506.5 1.3 collective-permute-start
  507.8 6.2 %collective-permute-done = f32[2]{0:T(128)S(1)} collective-permute-done((f32[2]{0:T(128)S(1)}, f32[2]{0:T(128)S(1)}, u32[]{:S(2)}, u32[]{:S(2)}) %collective-permute-start) | collective-permute-done | bytes 40 | tf_op jit(solution)/shard_map/while/body/eval_jaxpr/ppermute | solution.py:20
  514.1 1.3 collective-permute-start
  515.4 6.2 %collective-permute-done = f32[2]{0:T(128)S(1)} collective-permute-done((f32[2]{0:T(128)S(1)}, f32[2]{0:T(128)S(1)}, u32[]{:S(2)}, u32[]{:S(2)}) %collective-permute-start) | collective-permute-done | bytes 40 | tf_op jit(solution)/shard_map/while/body/eval_jaxpr/ppermute | solution.py:20
  521.6 1.3 collective-permute-start
  522.9 6.2 %collective-permute-done = f32[2]{0:T(128)S(1)} collective-permute-done((f32[2]{0:T(128)S(1)}, f32[2]{0:T(128)S(1)}, u32[]{:S(2)}, u32[]{:S(2)}) %collective-permute-start) | collective-permute-done | bytes 40 | tf_op jit(solution)/shard_map/while/body/eval_jaxpr/ppermute | solution.py:20
  529.2 1.3 collective-permute-start
  530.5 6.2 %collective-permute-done = f32[2]{0:T(128)S(1)} collective-permute-done((f32[2]{0:T(128)S(1)}, f32[2]{0:T(128)S(1)}, u32[]{:S(2)}, u32[]{:S(2)}) %collective-permute-start) | collective-permute-done | bytes 40 | tf_op jit(solution)/shard_map/while/body/eval_jaxpr/ppermute | solution.py:20
  (655 shorter events, 17.9 us)
Async XLA Ops:
  7.2 97.6 %all-gather.16.cloned.1.call-start = ((), (), s32[]{:S(2)}) async-start(), calls=%async_computation | async-start | bytes 11141120 | tf_op jit(solution)/shard_map/all_gather | solution.py:62
  22.3 164.7 %all-gather.18.cloned.1.call-start = ((), (), s32[]{:S(2)}) async-start(), calls=%async_computation.1 | async-start | bytes 11141120 | tf_op jit(solution)/shard_map/all_gather | solution.py:62
  37.0 391.7 %collective-permute-start.1 = (f32[2,1]{1,0:T(2,128)}, f32[2,1]{1,0:T(2,128)S(1)}, u32[]{:S(2)}, u32[]{:S(2)}) collective-permute-start(f32[2,1]{1,0:T(2,128)} %bitcast.117), channel_id=1, source_target_pairs={{8,0},{16,8},{24,16},{32,24},{40,32},{48,40},{56,48},{64,56},{72,6... | collective-permute-start | bytes 32 | tf_op jit(solution)/shard_map/ppermute | solution.py:20
  187.0 17.3 %copy-start = (f32[2,512,1152]{2,1,0:T(8,128)S(1)}, f32[2,512,1152]{2,1,0:T(8,128)}, u32[]{:S(2)}) copy-start(f32[2,512,1152]{2,1,0:T(8,128)} %get-tuple-element.608) | copy-start | bytes 14155780
  204.4 224.4 %copy-start.1 = (f32[2,32]{1,0:T(2,128)S(1)}, f32[2,32]{1,0:T(2,128)}, u32[]{:S(2)}) copy-start(f32[2,32]{1,0:T(2,128)} %param.23) | copy-start | bytes 772
  204.4 224.4 %copy-start.2 = (s32[2,32]{1,0:T(2,128)S(1)}, s32[2,32]{1,0:T(2,128)}, u32[]{:S(2)}) copy-start(s32[2,32]{1,0:T(2,128)} %param.20) | copy-start | bytes 772
  204.4 224.4 %copy-start.3 = (s32[2,32]{1,0:T(2,128)S(1)}, s32[2,32]{1,0:T(2,128)}, u32[]{:S(2)}) copy-start(s32[2,32]{1,0:T(2,128)} %param.21) | copy-start | bytes 772
  204.4 224.4 %copy-start.4 = (f32[2,32]{1,0:T(2,128)S(1)}, f32[2,32]{1,0:T(2,128)}, u32[]{:S(2)}) copy-start(f32[2,32]{1,0:T(2,128)} %param.22) | copy-start | bytes 772
  433.7 5.4 collective-permute-start
  439.1 5.4 collective-permute-start
  444.6 5.4 collective-permute-start
  450.0 5.4 collective-permute-start
  455.4 5.9 %collective-permute-start = (f32[2]{0:T(128)S(1)}, f32[2]{0:T(128)S(1)}, u32[]{:S(2)}, u32[]{:S(2)}) collective-permute-start(f32[2]{0:T(128)S(1)} %multiply_add_fusion.3), channel_id=1, source_target_pairs={{8,0},{16,8},{24,16},{32,24},{40,32},{48,40},{56,48},{64,56},{72,6... | collective-permute-start | bytes 32 | tf_op jit(solution)/shard_map/while/body/eval_jaxpr/ppermute | solution.py:20
  461.3 7.5 %collective-permute-start = (f32[2]{0:T(128)S(1)}, f32[2]{0:T(128)S(1)}, u32[]{:S(2)}, u32[]{:S(2)}) collective-permute-start(f32[2]{0:T(128)S(1)} %multiply_add_fusion.3), channel_id=1, source_target_pairs={{8,0},{16,8},{24,16},{32,24},{40,32},{48,40},{56,48},{64,56},{72,6... | collective-permute-start | bytes 32 | tf_op jit(solution)/shard_map/while/body/eval_jaxpr/ppermute | solution.py:20
  468.9 7.5 %collective-permute-start = (f32[2]{0:T(128)S(1)}, f32[2]{0:T(128)S(1)}, u32[]{:S(2)}, u32[]{:S(2)}) collective-permute-start(f32[2]{0:T(128)S(1)} %multiply_add_fusion.3), channel_id=1, source_target_pairs={{8,0},{16,8},{24,16},{32,24},{40,32},{48,40},{56,48},{64,56},{72,6... | collective-permute-start | bytes 32 | tf_op jit(solution)/shard_map/while/body/eval_jaxpr/ppermute | solution.py:20
  476.4 7.5 %collective-permute-start = (f32[2]{0:T(128)S(1)}, f32[2]{0:T(128)S(1)}, u32[]{:S(2)}, u32[]{:S(2)}) collective-permute-start(f32[2]{0:T(128)S(1)} %multiply_add_fusion.3), channel_id=1, source_target_pairs={{8,0},{16,8},{24,16},{32,24},{40,32},{48,40},{56,48},{64,56},{72,6... | collective-permute-start | bytes 32 | tf_op jit(solution)/shard_map/while/body/eval_jaxpr/ppermute | solution.py:20
  483.9 7.5 %collective-permute-start = (f32[2]{0:T(128)S(1)}, f32[2]{0:T(128)S(1)}, u32[]{:S(2)}, u32[]{:S(2)}) collective-permute-start(f32[2]{0:T(128)S(1)} %multiply_add_fusion.3), channel_id=1, source_target_pairs={{8,0},{16,8},{24,16},{32,24},{40,32},{48,40},{56,48},{64,56},{72,6... | collective-permute-start | bytes 32 | tf_op jit(solution)/shard_map/while/body/eval_jaxpr/ppermute | solution.py:20
  491.5 7.5 %collective-permute-start = (f32[2]{0:T(128)S(1)}, f32[2]{0:T(128)S(1)}, u32[]{:S(2)}, u32[]{:S(2)}) collective-permute-start(f32[2]{0:T(128)S(1)} %multiply_add_fusion.3), channel_id=1, source_target_pairs={{8,0},{16,8},{24,16},{32,24},{40,32},{48,40},{56,48},{64,56},{72,6... | collective-permute-start | bytes 32 | tf_op jit(solution)/shard_map/while/body/eval_jaxpr/ppermute | solution.py:20
  499.0 7.5 %collective-permute-start = (f32[2]{0:T(128)S(1)}, f32[2]{0:T(128)S(1)}, u32[]{:S(2)}, u32[]{:S(2)}) collective-permute-start(f32[2]{0:T(128)S(1)} %multiply_add_fusion.3), channel_id=1, source_target_pairs={{8,0},{16,8},{24,16},{32,24},{40,32},{48,40},{56,48},{64,56},{72,6... | collective-permute-start | bytes 32 | tf_op jit(solution)/shard_map/while/body/eval_jaxpr/ppermute | solution.py:20
  506.5 7.5 %collective-permute-start = (f32[2]{0:T(128)S(1)}, f32[2]{0:T(128)S(1)}, u32[]{:S(2)}, u32[]{:S(2)}) collective-permute-start(f32[2]{0:T(128)S(1)} %multiply_add_fusion.3), channel_id=1, source_target_pairs={{8,0},{16,8},{24,16},{32,24},{40,32},{48,40},{56,48},{64,56},{72,6... | collective-permute-start | bytes 32 | tf_op jit(solution)/shard_map/while/body/eval_jaxpr/ppermute | solution.py:20
  514.1 7.5 %collective-permute-start = (f32[2]{0:T(128)S(1)}, f32[2]{0:T(128)S(1)}, u32[]{:S(2)}, u32[]{:S(2)}) collective-permute-start(f32[2]{0:T(128)S(1)} %multiply_add_fusion.3), channel_id=1, source_target_pairs={{8,0},{16,8},{24,16},{32,24},{40,32},{48,40},{56,48},{64,56},{72,6... | collective-permute-start | bytes 32 | tf_op jit(solution)/shard_map/while/body/eval_jaxpr/ppermute | solution.py:20
  521.6 7.5 %collective-permute-start = (f32[2]{0:T(128)S(1)}, f32[2]{0:T(128)S(1)}, u32[]{:S(2)}, u32[]{:S(2)}) collective-permute-start(f32[2]{0:T(128)S(1)} %multiply_add_fusion.3), channel_id=1, source_target_pairs={{8,0},{16,8},{24,16},{32,24},{40,32},{48,40},{56,48},{64,56},{72,6... | collective-permute-start | bytes 32 | tf_op jit(solution)/shard_map/while/body/eval_jaxpr/ppermute | solution.py:20
  529.2 7.5 %collective-permute-start = (f32[2]{0:T(128)S(1)}, f32[2]{0:T(128)S(1)}, u32[]{:S(2)}, u32[]{:S(2)}) collective-permute-start(f32[2]{0:T(128)S(1)} %multiply_add_fusion.3), channel_id=1, source_target_pairs={{8,0},{16,8},{24,16},{32,24},{40,32},{48,40},{56,48},{64,56},{72,6... | collective-permute-start | bytes 32 | tf_op jit(solution)/shard_map/while/body/eval_jaxpr/ppermute | solution.py:20
Sparse Core Ops, SparseCore 0:
  22.4 82.3 all-gather.15
  106.9 80.0 all-gather.17
where the time goes:
time: 552 us; the launch traced here: 544 us
  blocking collectives  263 us (48%)
  waiting for transfers between devices  184 us (33%)
  matrix products  36.7 us (7%)
  starting transfers between devices  20.6 us (4%)
  other arithmetic  16.5 us (3%)
  between operations  14.2 us (3%)
    all_gather x6, blocking collectives, merged_2(): everything = jax.tree.map(lambda part: lax.all_gather(part, axis), x)  205 us
    all_gather x2, waiting for transfers between devices, body(): lax.all_gather((full_p, full_q), 'ctx', axis=1, tiled=True)  100 us
    ppermute x16, waiting for transfers between devices, from_behind(): lax.ppermute(value, axis, [(source, source + steps) for source in range(l...  83.5 us
    all_gather x1, blocking collectives, body(): ids_all = lax.all_gather(token_ids, 'ctx', axis=1, tiled=True)  28.1 us
    ppermute x16, starting transfers between devices, from_behind(): lax.ppermute(value, axis, [(source, source + steps) for source in range(l...  20.5 us
    dot_general x1, matrix products, body(): jnp.einsum('btd,dv->btv', piece_p, head_policy, preferred_element_type=jn...  19.3 us
    dot_general x1, matrix products, body(): jnp.einsum('btd,dv->btv', piece_q, head_ref, preferred_element_type=jnp.f...  17.3 us
    all_gather x1, blocking collectives, body(): lax.all_gather(hidden_policy, 'vocab', axis=2, tiled=True)  15.1 us
  transfers between devices with their start and end apart: 18, of which 17 were waited for; matrix products, arithmetic and copies ran while one was open for 10% of the time, Pallas kernels for 0%

commit v1 on v0

v1 whole, which is shorter than its diff:
```python
import jax
import jax.numpy as jnp
import numpy as np
from jax import lax
from jax.experimental import pallas as pl
from jax.experimental.pallas import tpu as pltpu
from jax.sharding import Mesh, PartitionSpec as P

PLANE = ("y", "z")
CHIPS = ("y", "z", "x")


def swap_cores(value):
    return lax.ppermute(value, "core", [(0, 1), (1, 0)])


def stats_kernel(ids_ref, hidden_ref, head_p_ref, head_q_ref, out_ref, acc_p, acc_q):
    step = pl.program_id(0)
    depth = hidden_ref.shape[-1]
    rows, width = acc_p.shape
    chunk = 128

    def add(acc, head_ref, first):
        tokens = hidden_ref.shape[-2]
        for r in range(0, rows, chunk):
            part = hidden_ref[pl.ds(r // tokens, chunk // tokens)].reshape(chunk, depth)
            product = jnp.dot(part, head_ref[...], preferred_element_type=jnp.float32)

            @pl.when(first)
            def _():
                acc[pl.ds(r, chunk), :] = product

            @pl.when(jnp.logical_not(first))
            def _():
                acc[pl.ds(r, chunk), :] += product

    @pl.when(step < 4)
    def _():
        add(acc_p, head_p_ref, step == 0)

    @pl.when(step >= 4)
    def _():
        add(acc_q, head_q_ref, step == 4)

    @pl.when(step == 7)
    def _():
        for r in range(0, rows, chunk):
            logits_p = acc_p[pl.ds(r, chunk), :]
            logits_q = acc_q[pl.ds(r, chunk), :]
            top_p = jnp.max(logits_p, axis=-1, keepdims=True)
            expo = jnp.exp(logits_p - top_p)
            sum_p = jnp.sum(expo, axis=-1, keepdims=True)
            cross = jnp.sum(expo * (logits_p - logits_q), axis=-1, keepdims=True)
            top_q = jnp.max(logits_q, axis=-1, keepdims=True)
            sum_q = jnp.sum(jnp.exp(logits_q - top_q), axis=-1, keepdims=True)
            column = lax.broadcasted_iota(jnp.int32, (chunk, width), 1)
            chosen = jnp.sum(
                jnp.where(column == ids_ref[pl.ds(r, chunk), :], logits_p, 0.0), axis=-1, keepdims=True
            )
            lane = lax.broadcasted_iota(jnp.int32, (chunk, 128), 1)
            packed = jnp.where(lane == 0, top_p + jnp.log(sum_p), 0.0)
            packed = jnp.where(lane == 1, cross / sum_p, packed)
            packed = jnp.where(lane == 2, top_q + jnp.log(sum_q), packed)
            packed = jnp.where(lane == 3, chosen, packed)
            out_ref[:, pl.ds(r, chunk)] = packed.T[0:8, :]


def block_stats(ids, hidden, head_p, head_q):
    blocks, _, _, tokens, depth = hidden.shape
    rows = blocks * tokens
    width = head_p.shape[1]
    return pl.pallas_call(
        stats_kernel,
        grid=(8,),
        in_specs=[
            pl.BlockSpec((rows, 1), lambda s: (0, 0)),
            pl.BlockSpec((blocks, None, None, tokens, depth), lambda s: (0, s % 4, s // 4, 0, 0)),
            pl.BlockSpec((depth, width), lambda s: (jnp.minimum(s, 3), 0)),
            pl.BlockSpec((depth, width), lambda s: (jnp.maximum(s - 4, 0), 0)),
        ],
        out_specs=pl.BlockSpec((8, rows), lambda s: (0, 0)),
        out_shape=jax.ShapeDtypeStruct((8, rows), jnp.float32),
        scratch_shapes=[pltpu.VMEM((rows, width), jnp.float32)] * 2,
        compiler_params=pltpu.CompilerParams(vmem_limit_bytes=48 << 20),
        cost_estimate=pl.CostEstimate(
            flops=4 * rows * 4 * depth * width,
            bytes_accessed=2 * 4 * depth * (width + rows) * 2,
            transcendentals=2 * rows * width,
        ),
        name="block_stats",
    )(ids, hidden, head_p, head_q)


def chain_products(coef):
    count = coef.shape[1]
    t = lax.broadcasted_iota(jnp.int32, (1, count, count), 1)
    u = lax.broadcasted_iota(jnp.int32, (1, count, count), 2)
    before = jnp.concatenate([jnp.ones_like(coef[:, :1]), coef[:, :-1]], axis=1)
    factors = jnp.where(u > t, before[:, None, :], 1.0)
    shift = 1
    while shift < count:
        moved = jnp.pad(factors[:, :, :-shift], ((0, 0), (0, 0), (shift, 0)), constant_values=1.0)
        factors = factors * moved
        shift *= 2
    return jnp.where(u >= t, factors, 0.0)


def body(hidden_policy, hidden_ref, head_policy, head_ref, token_ids, response_mask, done_flags, scores, values):
    y, z, x, core = (lax.axis_index(a) for a in ("y", "z", "x", "core"))
    width = head_policy.shape[1]
    tok = token_ids.shape[1]
    ctx = y * 4 + z
    first = core == 0

    def mine(pair):
        return jnp.where(first, pair[0], pair[1])

    def other(pair):
        return jnp.where(first, pair[1], pair[0])

    both = jnp.stack([hidden_policy, hidden_ref], axis=1)
    kept, given = mine(both), other(both)
    got = swap_cores(given)
    halves = jnp.concatenate([jnp.where(first, kept, got), jnp.where(first, got, kept)], axis=-1)
    hidden = lax.all_gather(halves, CHIPS)
    hidden = hidden.reshape((16, 4) + halves.shape)

    other_p, other_q = swap_cores(head_policy), swap_cores(head_ref)

    mask = response_mask.astype(jnp.float32)
    done = done_flags.astype(jnp.float32)
    coef = 0.998 * (1.0 - done)
    products = chain_products(coef)
    decay = products[:, :, -1] * coef[:, -1:]
    shared = jnp.concatenate(
        [token_ids.astype(jnp.float32), decay[:, :1], values[:, :1], jnp.zeros((2, 30), jnp.float32)], axis=1
    )
    shared = lax.all_to_all(jnp.broadcast_to(shared.reshape(1, 128), (16, 128)), PLANE, 0, 0, tiled=True)
    shared = shared.reshape(16, 2, 64)
    ids = mine(jnp.moveaxis(shared[:, :, :tok], 1, 0)).reshape(16 * tok).astype(jnp.int32)
    place = lax.broadcasted_iota(jnp.int32, (1, 16), 1)
    head_decay = shared[:, :, tok].T
    first_value = shared[:, :, tok + 1].T
    following = jnp.sum(jnp.where(place == ctx + 1, first_value, 0.0), axis=1, keepdims=True)
    next_value = jnp.concatenate([values[:, 1:], following], axis=1)
    known = done * scores + (1.0 - done) * next_value - values
    later = chain_products(head_decay)
    weights = jnp.sum(
        jnp.where(lax.broadcasted_iota(jnp.int32, (1, 16, 1), 1) == ctx + 1, later, 0.0), axis=1
    )

    columns = (ctx * 8 + x * 2) * width
    parts = []
    for k, heads in ((core, (head_policy, head_ref)), (1 - core, (other_p, other_q))):
        local = (ids - (columns + k * width))[:, None]
        parts.append(block_stats(local, hidden, *heads)[:4])
    stats = jnp.stack(parts).reshape(2, 4, 16, tok).transpose(2, 1, 0, 3).reshape(16, 1, 8 * tok)
    stats = jnp.broadcast_to(stats, (16, 4, 8 * tok)).reshape(64, 8 * tok)
    stats = lax.all_to_all(stats, CHIPS, 0, 0, tiled=True)
    stats = stats.reshape(64, 4, 2, tok)
    lse_p, ratio, lse_q, chosen = (stats[:, i] for i in range(4))
    top_p = jnp.max(lse_p, axis=(0, 1))
    w_p = jnp.exp(lse_p - top_p)
    total = jnp.sum(w_p, axis=(0, 1))
    lz_p = top_p + jnp.log(total)
    top_q = jnp.max(lse_q, axis=(0, 1))
    lz_q = top_q + jnp.log(jnp.sum(jnp.exp(lse_q - top_q), axis=(0, 1)))
    kl_val = jnp.sum(w_p * ratio, axis=(0, 1)) / total - lz_p + lz_q
    logprobs = jnp.sum(chosen, axis=(0, 1)) - lz_p
    penalty = -0.05 * mine(mask) * kl_val
    rewards = penalty + mine(done * scores)
    delta = penalty + mine(known)
    local_gae = jnp.sum(mine(products) * delta[None, :], axis=1)
    heads = lax.all_to_all(jnp.broadcast_to(local_gae[:1], (16, 1)), PLANE, 0, 0, tiled=True)
    incoming = jnp.sum(mine(weights) * heads[:, 0])
    gae = local_gae + mine(decay) * incoming
    own = jnp.stack([rewards, mine(mask) * gae, mine(mask) * (gae + mine(values)), logprobs])
    theirs = swap_cores(own)
    return tuple(
        jnp.stack([jnp.where(first, own[i], theirs[i]), jnp.where(first, theirs[i], own[i])]) for i in range(4)
    )


def solution(mesh):
    fine = Mesh(np.asarray(mesh.devices).reshape(4, 4, 4, 2), ("y", "z", "x", "core"))
    vocab = ("x", "core")
    placed = (
        P(None, PLANE, vocab),
        P(None, PLANE, vocab),
        P(None, PLANE + vocab),
        P(None, PLANE + vocab),
        P(None, PLANE),
        P(None, PLANE),
        P(None, PLANE),
        P(None, PLANE),
        P(None, PLANE),
    )
    return jax.shard_map(
        body,
        mesh=fine,
        in_specs=placed,
        out_specs=(P(None, PLANE),) * 4,
        check_vma=False,
    )
```

time: 552 us -> 198 us (0.36); the launches traced: 544 us -> 197 us
  blocking collectives: 263 us -> 0 us
  waiting for transfers between devices: 184 us -> 90 us
  Pallas kernels: 0 us -> 54 us
  matrix products: 36.7 us -> 0 us
    all_gather x9 -> x0, blocking collectives: 263 us -> none  [the longest x6 205 us: merged_2(): everything = jax.tree.map(lambda part: lax.all_gather(part, axis), x)]
    ppermute x16 -> x4, waiting for transfers between devices: 83.5 us -> 2.41 us  [swap_cores(): return lax.ppermute(value, 'core', [(0, 1), (1, 0)])]
    pallas_call x0 -> x2, Pallas kernels: none -> 54 us  [block_stats(): pl.pallas_call(stats_kernel, grid=(8,), in_specs=[pl.BlockSpec((rows, 1),...]
    dot_general x2 -> x0, matrix products: 36.7 us -> none  [the longest x1 19.3 us: body(): jnp.einsum('btd,dv->btv', piece_p, head_policy, preferred_element_type=jn...]
    all_gather x2 -> x1, waiting for transfers between devices: 100 us -> 64.5 us  [body(): hidden = lax.all_gather(halves, CHIPS)]
    all_to_all x0 -> x3, waiting for transfers between devices: none -> 23 us  [the longest x1 9.49 us: body(): stats = lax.all_to_all(stats, CHIPS, 0, 0, tiled=True)]
    all_to_all x0 -> x3, starting transfers between devices: none -> 20.2 us  [the longest x1 8.62 us: body(): stats = lax.all_to_all(stats, CHIPS, 0, 0, tiled=True)]
    ppermute x16 -> x4, starting transfers between devices: 20.5 us -> 0.76 us  [swap_cores(): return lax.ppermute(value, 'core', [(0, 1), (1, 0)])]
  transfers between devices with their start and end apart: 18 -> 8, of which waited for: 17 -> 6; matrix products, arithmetic and copies ran while one was open for 10% -> 4% of each run, Pallas kernels for 0% -> 14%
where the time goes in v1:
time: 198 us; the launch traced here: 197 us
  waiting for transfers between devices  90 us (45%)
  Pallas kernels  54 us (27%)
  starting transfers between devices  21 us (11%)
  between operations  14.4 us (7%)
  other arithmetic  12.1 us (6%)
  local copies, waits for them, and re-layouts  5.2 us (3%)
    all_gather x1, waiting for transfers between devices, body(): hidden = lax.all_gather(halves, CHIPS)  64.5 us
    pallas_call x2, Pallas kernels, block_stats(): pl.pallas_call(stats_kernel, grid=(8,), in_specs=[pl.BlockSpec((rows, 1),...  54 us
    all_to_all x1, waiting for transfers between devices, body(): stats = lax.all_to_all(stats, CHIPS, 0, 0, tiled=True)  9.49 us
    all_to_all x1, starting transfers between devices, body(): stats = lax.all_to_all(stats, CHIPS, 0, 0, tiled=True)  8.62 us
    all_to_all x1, starting transfers between devices, body(): lax.all_to_all(jnp.broadcast_to(shared.reshape(1, 128), (16, 128)), PLANE...  8.13 us
    all_to_all x1, waiting for transfers between devices, body(): lax.all_to_all(jnp.broadcast_to(local_gae[:1], (16, 1)), PLANE, 0, 0, til...  7.48 us
    all_to_all x1, waiting for transfers between devices, body(): lax.all_to_all(jnp.broadcast_to(shared.reshape(1, 128), (16, 128)), PLANE...  6.04 us
  transfers between devices with their start and end apart: 8, of which 6 were waited for; matrix products, arithmetic and copies ran while one was open for 4% of the time, Pallas kernels for 14%

profile of v1, /device:TPU:0, one launch (start us, length us, event | category | flops | bytes accessed | tf_op | source)
XLA Modules:
  0.0 196.7 jit_solution(12149728141699523205)
XLA Ops:
  7.2 0.9 select_bitcast_fusion
  8.2 1.3 collective-permute-done
  9.4 0.9 bitcast_select_fusion.1
  10.4 0.7 pad_maximum_fusion
  11.1 0.2 collective-permute-start.1
  11.3 0.4 collective-permute-start.2
  11.6 0.7 convert_element_type.25
  12.3 0.7 fusion.12
  13.0 0.1 copy.78
  13.1 0.1 broadcast_select_fusion.2
  13.2 0.1 pad_multiply_fusion.3
  13.4 0.1 pad_multiply_fusion.2
  13.6 0.2 slice_reduce_fusion.3
  14.0 0.8 maximum_maximum_fusion
  14.8 0.6 broadcast_in_dim.123
  15.4 8.1 %all-to-all-start = ((f32[16,1,128]{2,1,0:T(1,128)}), f32[16,1,128]{2,1,0:T(1,128)S(1)}, u32[]{:S(2)}, u32[]{:S(2)}) async-start(f32[16,1,128]{2,1,0:T(1,128)} %broadcast_in_dim.123), calls=%async_computation | async-start | bytes 16384 | tf_op jit(solution)/shard_map/all_to_all | solution.py:138
  23.6 0.8 slice.182
  24.4 0.7 convert_element_type.24
  25.0 6.0 %all-to-all-done = f32[16,1,128]{2,1,0:T(1,128)S(1)} async-done(((f32[16,1,128]{2,1,0:T(1,128)}), f32[16,1,128]{2,1,0:T(1,128)S(1)}, u32[]{:S(2)}, u32[]{:S(2)}) %all-to-all-start) | async-done | bytes 8224 | tf_op jit(solution)/shard_map/all_to_all | solution.py:138
  31.1 0.5 broadcast.144
  31.6 0.7 reduce.18
  32.7 0.1 fusion.11
  32.8 0.1 copy.76
  33.0 0.3 sub.103.ids_ref
  33.3 0.3 sub.104.ids_ref
  33.5 0.8 convert_multiply_fusion
  34.6 64.5 %all-gather.3.cloned.1.call-done = bf16[128,32,1280]{2,1,0:T(8,128)(2,1)} async-done(((bf16[2,32,1280]{2,1,0:T(8,128)(2,1)}), bf16[128,32,1280]{2,1,0:T(8,128)(2,1)}) %all-gather.3.cloned.1.call-update) | async-done | bytes 10485776 | tf_op jit(solution)/shard_map/all_gather | solution.py:125
  99.1 26.9 %block_stats.2 = f32[8,512]{1,0:T(8,128)S(1)} custom-call(s32[512,1]{1,0:T(8,128)S(1)} %sub.103.ids_ref, bf16[16,4,2,32,1280]{4,3,2,1,0:T(8,128)(2,1)} %bitcast.90, bf16[5120,1152]{1,0:T(8,128)(2,1)} %head_p_ref.1, bf16[5120,1152]{1,0:T(8,128)(2,1)} %head_q_ref.1), custom_call_target="tpu_custom_call" | custom-call | flops 12079595520 | bytes 34078720 | tf_op jit(solution)/shard_map/block_stats/pallas_call | solution.py:72
  126.2 27.1 %block_stats.3 = f32[8,512]{1,0:T(8,128)S(1)} custom-call(s32[512,1]{1,0:T(8,128)S(1)} %sub.104.ids_ref, bf16[16,4,2,32,1280]{4,3,2,1,0:T(8,128)(2,1)} %bitcast.91, bf16[5120,1152]{1,0:T(8,128)(2,1)} %collective-permute-done.1.head_p_ref, bf16[5120,1152]{1,0:T(8,128)(2,1)} %collective-permute-done.2.head_q_ref), custom_call_target="tpu_custom_call" | custom-call | flops 12079595520 | bytes 34078720 | tf_op jit(solution)/shard_map/block_stats/pallas_call | solution.py:72
  153.5 0.1 broadcast_in_dim.124
  153.7 0.7 all_to_all.18
  154.4 8.6 %all-to-all-start.1 = ((f32[64,1,256]{2,1,0:T(1,128)}), f32[64,1,256]{2,1,0:T(1,128)S(1)}, u32[]{:S(2)}, u32[]{:S(2)}) async-start(f32[64,1,256]{2,1,0:T(1,128)} %all_to_all.18), calls=%async_computation.1 | async-start | bytes 131072 | tf_op jit(solution)/shard_map/all_to_all | solution.py:159
  163.0 0.1 select_reduce_fusion
  163.1 9.5 %all-to-all-done.1 = f32[64,1,256]{2,1,0:T(1,128)S(1)} async-done(((f32[64,1,256]{2,1,0:T(1,128)}), f32[64,1,256]{2,1,0:T(1,128)S(1)}, u32[]{:S(2)}, u32[]{:S(2)}) %all-to-all-start.1) | async-done | bytes 65568 | tf_op jit(solution)/shard_map/all_to_all | solution.py:159
  172.6 0.1 copy.74
  172.7 0.2 slice_reduce_fusion
  172.8 0.2 fusion.6
  173.2 0.6 broadcast_in_dim.135
  173.8 3.5 %all-to-all-start.2 = ((f32[16,1,1]{2,1,0:T(1,128)}), f32[16,1,1]{2,1,0:T(1,128)S(1)}, u32[]{:S(2)}, u32[]{:S(2)}) async-start(f32[16,1,1]{2,1,0:T(1,128)} %broadcast_in_dim.135), calls=%async_computation.2 | async-start | bytes 16384 | tf_op jit(solution)/shard_map/all_to_all | solution.py:174
  177.3 7.5 %all-to-all-done.2 = f32[16,1,1]{2,1,0:T(1,128)S(1)} async-done(((f32[16,1,1]{2,1,0:T(1,128)}), f32[16,1,1]{2,1,0:T(1,128)S(1)}, u32[]{:S(2)}, u32[]{:S(2)}) %all-to-all-start.2) | async-done | bytes 96 | tf_op jit(solution)/shard_map/all_to_all | solution.py:174
  184.8 0.2 reduce.8
  185.0 0.6 fusion.22
  185.6 0.7 fusion.23
  186.4 1.1 collective-permute-done.3
  187.6 0.6 pad_maximum_fusion.6
  188.1 0.6 pad_maximum_fusion.3
  188.7 0.6 pad_maximum_fusion.4
  189.3 0.6 pad_maximum_fusion.5
  (52 shorter events, 1.9 us)
Async XLA Ops:
  7.2 91.9 %all-gather.3.cloned.1.call-start = ((), (), s32[]{:S(2)}) async-start(), calls=%async_computation.3 | async-start | bytes 10649600 | tf_op jit(solution)/shard_map/all_gather | solution.py:125
  8.1 1.4 collective-permute-start
  11.1 115.1 %collective-permute-start.1 = (bf16[5120,1152]{1,0:T(8,128)(2,1)}, bf16[5120,1152]{1,0:T(8,128)(2,1)}, u32[]{:S(2)}, u32[]{:S(2)}) collective-permute-start(bf16[5120,1152]{1,0:T(8,128)(2,1)} %head_p_ref.1), channel_id=1, source_target_pairs={{0,1},{1,0},{2,3},{3,2},{4,5},{5,4},{6,7},{7,6},{8,9},{9,8},{10,11... | collective-permute-start | bytes 35389448 | tf_op jit(solution)/shard_map/ppermute | solution.py:14
  11.3 114.9 %collective-permute-start.2 = (bf16[5120,1152]{1,0:T(8,128)(2,1)}, bf16[5120,1152]{1,0:T(8,128)(2,1)}, u32[]{:S(2)}, u32[]{:S(2)}) collective-permute-start(bf16[5120,1152]{1,0:T(8,128)(2,1)} %head_q_ref.1), channel_id=1, source_target_pairs={{0,1},{1,0},{2,3},{3,2},{4,5},{5,4},{6,7},{7,6},{8,9},{9,8},{10,11... | collective-permute-start | bytes 35389448 | tf_op jit(solution)/shard_map/ppermute | solution.py:14
  15.4 15.7 %all-to-all-start = ((f32[16,1,128]{2,1,0:T(1,128)}), f32[16,1,128]{2,1,0:T(1,128)S(1)}, u32[]{:S(2)}, u32[]{:S(2)}) async-start(f32[16,1,128]{2,1,0:T(1,128)} %broadcast_in_dim.123), calls=%async_computation | async-start | bytes 16384 | tf_op jit(solution)/shard_map/all_to_all | solution.py:138
  126.1 60.1 %copy-start = (f32[2,32]{1,0:T(2,128)S(1)}, f32[2,32]{1,0:T(2,128)}, u32[]{:S(2)}) copy-start(f32[2,32]{1,0:T(2,128)} %param.17) | copy-start | bytes 772
  154.4 18.2 %all-to-all-start.1 = ((f32[64,1,256]{2,1,0:T(1,128)}), f32[64,1,256]{2,1,0:T(1,128)S(1)}, u32[]{:S(2)}, u32[]{:S(2)}) async-start(f32[64,1,256]{2,1,0:T(1,128)} %all_to_all.18), calls=%async_computation.1 | async-start | bytes 131072 | tf_op jit(solution)/shard_map/all_to_all | solution.py:159
  173.8 11.0 %all-to-all-start.2 = ((f32[16,1,1]{2,1,0:T(1,128)}), f32[16,1,1]{2,1,0:T(1,128)S(1)}, u32[]{:S(2)}, u32[]{:S(2)}) async-start(f32[16,1,1]{2,1,0:T(1,128)} %broadcast_in_dim.135), calls=%async_computation.2 | async-start | bytes 16384 | tf_op jit(solution)/shard_map/all_to_all | solution.py:174
  186.3 1.2 collective-permute-start.3
Sparse Core Ops, SparseCore 0:
  11.2 87.8 all-gather.2

commit v2 on v1

v2 whole, which is shorter than its diff:
```python
import functools

import jax
import jax.numpy as jnp
import numpy as np
from jax import lax
from jax.experimental import pallas as pl
from jax.experimental.pallas import tpu as pltpu
from jax.sharding import Mesh, PartitionSpec as P


PLANE = ("y", "z")
VOCAB = ("x", "core")
ALL = PLANE + VOCAB
SHARED = 16
HALF = (64 - SHARED) // 2
STARTS = (SHARED, SHARED + HALF)
TILE = 256


def swap_cores(value):
    return lax.ppermute(value, "core", [(0, 1), (1, 0)])


def near(value, axis):
    pairs = [(2 * i + c, 2 * ((i + (1, 3)[c]) % 4) + c) for i in range(4) for c in range(2)]
    return lax.ppermute(value, (axis, "core"), pairs)


def far(value, axis):
    pairs = [(2 * i + c, 2 * ((i + 2) % 4) + c) for i in range(4) for c in range(2)]
    return lax.ppermute(value, (axis, "core"), pairs)


def block_products(m, blocks, chunks, head, logits, fresh):
    width = logits.shape[2]
    top = 0
    for count, piece in chunks:
        parts = [piece(m, j) for j in blocks]
        for start in range(0, width, TILE):
            end = min(start + TILE, width)
            product = sum(
                jnp.dot(part, head[j * 1280 : (j + 1) * 1280, start:end], preferred_element_type=jnp.float32)
                for j, part in zip(blocks, parts)
            )
            if fresh:
                logits[m, top : top + count, start:end] = product
            else:
                logits[m, top : top + count, start:end] += product
        top += count


def row_stats(logits, ids, packed):
    chunk = 64
    lane = lax.broadcasted_iota(jnp.int32, (chunk, 128), 1)
    tiles = range(0, logits.shape[2], 128)

    def finish(i, carry):
        here = pl.ds(pl.multiple_of(i * chunk, chunk), chunk)
        top_p = jnp.max(
            functools.reduce(jnp.maximum, [logits[0, here, t : t + 128] for t in tiles]), axis=-1, keepdims=True
        )
        top_q = jnp.max(
            functools.reduce(jnp.maximum, [logits[1, here, t : t + 128] for t in tiles]), axis=-1, keepdims=True
        )
        relative = None if ids is None else ids[here, :] - lane
        sums = None
        for t in tiles:
            p, q = logits[0, here, t : t + 128], logits[1, here, t : t + 128]
            expo = jnp.exp(p - top_p)
            terms = expo, expo * (p - q), jnp.exp(q - top_q)
            if ids is not None:
                terms += (jnp.where(relative == t, p, 0.0),)
            sums = terms if sums is None else tuple(a + b for a, b in zip(sums, terms))
        sum_p, cross, sum_q, *chosen = (jnp.sum(v, axis=-1, keepdims=True) for v in sums)
        found = jnp.where(lane == 0, top_p + jnp.log(sum_p), 0.0)
        found = jnp.where(lane == 1, cross / sum_p, found)
        found = jnp.where(lane == 2, top_q + jnp.log(sum_q), found)
        packed[here, :] = jnp.where(lane == 3, chosen[0], found) if chosen else found
        return carry

    lax.fori_loop(0, logits.shape[1] // chunk, finish, 0)


def near_blocks(where_ref):
    x = where_ref[2]
    return [lax.rem(x + d, 4) for d in (0, 3, 1, 2)]


def placed_blocks(places, where_ref):
    y, z, core = where_ref[0], where_ref[1], where_ref[3]
    blocks = []
    for kind, by_core in places:
        for (along_0, across_0), (along_1, across_1) in zip(*by_core):
            along = jnp.where(core == 0, along_0, along_1)
            across = jnp.where(core == 0, across_0, across_1)
            dy, dz = (along, across) if kind == 0 else (across, along)
            ctx = lax.rem(y + dy, 4) * 4 + lax.rem(z + dz, 4)
            blocks.append((ctx, STARTS[kind]))
    return blocks


def moved_chunks(refs):
    def chunk(some):
        return 2 * HALF * len(some), lambda m, j: jnp.concatenate([ref[m, j] for ref in some], axis=0)

    return [chunk(refs[i : i + 4]) for i in range(0, len(refs), 4)]


def take_ids(blocks, ids_ref, ids):
    for i, (ctx, start) in enumerate(blocks):
        ids[i * HALF : (i + 1) * HALF, :] = ids_ref[ctx, start : start + HALF, :]


def give_stats(blocks, found, out_ref):
    for i, (ctx, start) in enumerate(blocks):
        out_ref[ctx, :, start : start + HALF] = found[:, i * HALF : (i + 1) * HALF]


def chosen_logits(logits, ids, packed):
    chunk = 64
    lane = lax.broadcasted_iota(jnp.int32, (chunk, 128), 1)

    def pick(i, carry):
        here = pl.ds(pl.multiple_of(i * chunk, chunk), chunk)
        relative = ids[here, :] - lane
        total = sum(
            jnp.where(relative == t, logits[here, t : t + 128], 0.0) for t in range(0, logits.shape[1], 128)
        )
        packed[here, :] = jnp.where(lane == 3, jnp.sum(total, axis=-1, keepdims=True), 0.0)
        return carry

    lax.fori_loop(0, logits.shape[0] // chunk, pick, 0)


class HeadBlocks:
    ahead = 4

    def __init__(self, heads, near_to, buffer, sems):
        self.order = [(m, j) for m in range(2) for j in range(4)]
        self.copies = [
            pltpu.make_async_copy(
                heads[m].at[pl.ds(pl.multiple_of(near_to[j] * 1280, 1280), 1280)],
                buffer.at[m, pl.ds(j * 1280, 1280)],
                sems.at[m, j],
            )
            for m, j in self.order
        ]
        for copy in self.copies[: self.ahead]:
            copy.start()

    def wait(self, k):
        self.copies[k].wait()
        if k + self.ahead < len(self.copies):
            self.copies[k + self.ahead].start()


def early_kernel(places, where_ref, *refs):
    count = len(places)
    moved, heads = refs[:count], refs[count : count + 2]
    out_ref, logits_ref, packed, logits, buffer, sems = refs[count + 2 :]
    stream = HeadBlocks(heads, near_blocks(where_ref), buffer, sems)
    chunks = moved_chunks(moved)
    for i in range(0, 8, 2):
        m, j = stream.order[i]
        stream.wait(i)
        stream.wait(i + 1)
        block_products(m, (j, j + 1), chunks, buffer.at[m], logits, j == 0)
    row_stats(logits, None, packed)
    logits_ref[...] = logits[0]
    give_stats(placed_blocks(places, where_ref), packed[...].T[0:8], out_ref)


def late_kernel(places, earlier, where_ref, ids_ref, *refs):
    count = len(places)
    moved, source, heads, earlier_logits = refs[:count], refs[count], refs[count + 1 : count + 3], refs[count + 3]
    out_ref, packed, logits, buffer, sems, hidden, hidden_sems, ids = refs[-8:]
    near_to = near_blocks(where_ref)
    stream = HeadBlocks(heads, near_to, buffer, sems)
    shared = [
        pltpu.make_async_copy(source.at[:, near_to[j], :, pl.ds(0, 2 * SHARED)], hidden.at[j], hidden_sems.at[j])
        for j in range(4)
    ]
    for copy in shared:
        copy.start()
    before = placed_blocks(earlier, where_ref)
    take_ids(before, ids_ref, ids)
    chosen_logits(earlier_logits, ids, packed)
    found = packed[...].T[0:8]
    for i, (ctx, start) in enumerate(before):
        out_ref[ctx, 3:4, start : start + HALF] = found[3:4, i * HALF : (i + 1) * HALF]

    blocks = placed_blocks(places, where_ref)
    first, rows = HALF * len(blocks), 16 * SHARED
    take_ids(blocks, ids_ref, ids)
    ids[first : first + rows, :] = ids_ref[:, 0:SHARED, :].reshape(rows, 1)

    def piece(m, j):
        halves = [hidden[j, :, c, m * SHARED : (m + 1) * SHARED].reshape(rows, 640) for c in range(2)]
        return jnp.concatenate(halves, axis=1)

    chunks = moved_chunks(moved) + [(rows, piece)]
    for i in range(0, 8, 2):
        m, j = stream.order[i]
        for k in (i, i + 1):
            stream.wait(k)
            if m == 0:
                shared[k].wait()
        block_products(m, (j, j + 1), chunks, buffer.at[m], logits, j == 0)
    row_stats(logits, ids, packed)
    found = packed[...].T[0:8]
    give_stats(blocks, found, out_ref)
    for ctx in range(16):
        out_ref[ctx, :, 0:SHARED] = found[:, first + ctx * SHARED : first + (ctx + 1) * SHARED]


def stats_call(kernel, name, rows, operands, spaces, heads, outs, scratch, aliases):
    depth, width = heads[0].shape
    return pl.pallas_call(
        kernel,
        in_specs=[pl.BlockSpec(memory_space=space) for space in spaces],
        out_specs=[pl.BlockSpec(memory_space=pltpu.VMEM)] * len(outs),
        out_shape=outs,
        scratch_shapes=[
            pltpu.VMEM((rows, 128), jnp.float32),
            pltpu.VMEM((2, rows, width), jnp.float32),
            pltpu.VMEM((2, depth, width), jnp.bfloat16),
            pltpu.SemaphoreType.DMA((2, 4)),
        ]
        + scratch,
        input_output_aliases=aliases,
        compiler_params=pltpu.CompilerParams(vmem_limit_bytes=47 << 20),
        cost_estimate=pl.CostEstimate(flops=1, bytes_accessed=1, transcendentals=0),
        name=name,
    )(*operands)


def early_stats(where, pieces, heads):
    rows = 2 * HALF * len(pieces)
    return stats_call(
        functools.partial(early_kernel, tuple(p for _, p in pieces)),
        "early_stats",
        rows,
        (where, *[a for a, _ in pieces], *heads),
        [pltpu.SMEM] + [pltpu.VMEM] * len(pieces) + [pltpu.HBM] * 2,
        heads,
        [
            jax.ShapeDtypeStruct((16, 8, 128), jnp.float32),
            jax.ShapeDtypeStruct((rows, heads[0].shape[1]), jnp.float32),
        ],
        [],
        {},
    )


def late_stats(where, ids, pieces, gathered, heads, earlier, earlier_logits, stats):
    rows = 2 * HALF * len(pieces) + 16 * SHARED
    operands = (where, ids, *[a for a, _ in pieces], gathered, *heads, earlier_logits, stats)
    return stats_call(
        functools.partial(late_kernel, tuple(p for _, p in pieces), tuple(p for _, p in earlier)),
        "late_stats",
        rows,
        operands,
        [pltpu.SMEM] + [pltpu.VMEM] * (1 + len(pieces)) + [pltpu.HBM] * 3 + [pltpu.VMEM] * 2,
        heads,
        [jax.ShapeDtypeStruct(stats.shape, stats.dtype)],
        [
            pltpu.VMEM((4, 16, 2, 2 * SHARED, 640), jnp.bfloat16),
            pltpu.SemaphoreType.DMA((4,)),
            pltpu.VMEM((rows, 1), jnp.int32),
        ],
        {len(operands) - 1: 0},
    )[0]


def chain_products(coef):
    count = coef.shape[1]
    t = lax.broadcasted_iota(jnp.int32, (1, count, count), 1)
    u = lax.broadcasted_iota(jnp.int32, (1, count, count), 2)
    before = jnp.concatenate([jnp.ones_like(coef[:, :1]), coef[:, :-1]], axis=1)
    factors = jnp.where(u > t, before[:, None, :], 1.0)
    shift = 1
    while shift < count:
        moved = jnp.pad(factors[:, :, :-shift], ((0, 0), (0, 0), (shift, 0)), constant_values=1.0)
        factors = factors * moved
        shift *= 2
    return jnp.where(u >= t, factors, 0.0)


def split_exact(value):
    parts = []
    for _ in range(3):
        part = lax.reduce_precision(value, 8, 7)
        parts.append(part)
        value = value - part
    return parts


def gather_line(first, value, axis):
    beside, across = near(value, axis), far(jnp.where(first, value[0], value[1]), axis)
    beside_2, across_2 = swap_cores(beside), swap_cores(across)
    before = jnp.where(first, beside, beside_2)
    after = jnp.where(first, beside_2, beside)
    opposite = jnp.stack([jnp.where(first, across, across_2), jnp.where(first, across_2, across)])
    return value, before, after, opposite


def body(hidden_policy, hidden_ref, head_policy, head_ref, token_ids, response_mask, done_flags, scores, values):
    y, z, x, core = (lax.axis_index(a) for a in ALL)
    width = head_policy.shape[1]
    tok = token_ids.shape[1]
    ctx = y * 4 + z
    first = core == 0
    where = jnp.stack([y, z, x, core])
    heads = (head_policy, head_ref)

    both = jnp.stack([hidden_policy.reshape(64, 640), hidden_ref.reshape(64, 640)])
    rest = both[:, SHARED:]
    got = swap_cores(rest)
    rest = jnp.concatenate([jnp.where(first, rest, got), jnp.where(first, got, rest)], axis=-1)

    mask = response_mask.astype(jnp.float32)
    done = done_flags.astype(jnp.float32)
    coef = 0.998 * (1.0 - done)
    products = chain_products(coef)
    decay = products[:, :, -1] * coef[:, -1:]

    digits = [token_ids & 255, (token_ids >> 8) & 255, token_ids >> 16]
    numbers = split_exact(jnp.stack([decay[:, 0], values[:, 0]]))
    extra = jnp.concatenate(
        [d.reshape(64).astype(jnp.bfloat16) for d in digits] + [n.reshape(4).astype(jnp.bfloat16) for n in numbers]
    )
    extra = jnp.pad(extra[None], ((0, 7), (0, 640 - extra.shape[0])))
    gathered = lax.all_gather(jnp.concatenate([both[:, :SHARED].reshape(2 * SHARED, 640), extra]), ALL)
    gathered = gathered.reshape(16, 4, 2, 2 * SHARED + 8, 640)
    extra = gathered[:, 0, 0, 2 * SHARED, :256].astype(jnp.float32)
    ids = (extra[:, :64] + 256.0 * extra[:, 64:128] + 65536.0 * extra[:, 128:192]).astype(jnp.int32)
    ids = (ids - (ctx * 8 + x * 2 + core) * width)[:, :, None]
    numbers = extra[:, 192:196] + extra[:, 196:200] + extra[:, 200:204]
    head_decay, first_value = numbers[:, :2].T, numbers[:, 2:].T

    line = jnp.stack(gather_line(first, rest, "x"), axis=1)
    arrays = []
    for kind, (axis_2, axis_3) in enumerate((("z", "y"), ("y", "z"))):
        own, before, after, opposite = gather_line(first, line[:, :, kind * HALF : (kind + 1) * HALF], axis_2)
        lower = jnp.concatenate([own, before], axis=2)
        upper = jnp.concatenate([after, opposite], axis=2)
        arrays.append((jnp.where(first, lower, upper), jnp.where(first, upper, lower), axis_3))

    place = lax.broadcasted_iota(jnp.int32, (1, 16), 1)
    following = jnp.sum(jnp.where(place == ctx + 1, first_value, 0.0), axis=1, keepdims=True)
    next_value = jnp.concatenate([values[:, 1:], following], axis=1)
    known = done * scores + (1.0 - done) * next_value - values
    later = chain_products(head_decay)
    weights = jnp.sum(jnp.where(lax.broadcasted_iota(jnp.int32, (1, 16, 1), 1) == ctx + 1, later, 0.0), axis=1)

    def place_of(kind, along, halves):
        across = (0, 3, 1, 2)
        return kind, tuple(
            tuple((along[c], s) for s in across[2 * halves[c] : 2 * halves[c] + 2]) for c in range(2)
        )

    ones, twos, axes = zip(*arrays)
    kinds = range(2)
    ones_1 = [near(ones[k], axes[k]) for k in kinds]
    twos_1 = [near(twos[k], axes[k]) for k in kinds]
    ones_2 = [near(ones_1[k], axes[k]) for k in kinds]
    others_1 = [swap_cores(ones_1[k]) for k in kinds]
    early = [(ones[k], place_of(k, (0, 0), (0, 1))) for k in kinds]
    early += [(twos[k], place_of(k, (0, 0), (1, 0))) for k in kinds]
    early += [(ones_1[k], place_of(k, (3, 1), (0, 1))) for k in kinds]
    early += [(others_1[k], place_of(k, (1, 3), (1, 0))) for k in kinds]
    stats, early_logits = early_stats(where, early, heads)
    *arrived, stats = lax.optimization_barrier((*twos_1, *ones_2, stats))
    twos_1, ones_2 = arrived[:2], arrived[2:]
    late = [(twos_1[k], place_of(k, (3, 1), (1, 0))) for k in kinds]
    late += [(swap_cores(twos_1[k]), place_of(k, (1, 3), (0, 1))) for k in kinds]
    late += [(ones_2[k], place_of(k, (2, 2), (0, 1))) for k in kinds]
    late += [(swap_cores(ones_2[k]), place_of(k, (2, 2), (1, 0))) for k in kinds]
    stats = late_stats(where, ids, late, gathered, heads, early, early_logits, stats)

    stats = jnp.broadcast_to(stats[:, :4, :64].reshape(16, 1, 256), (16, 8, 256)).reshape(128, 256)
    stats = lax.all_to_all(stats, ALL, 0, 0, tiled=True).reshape(128, 4, 2, tok)
    lse_p, ratio, lse_q, chosen = (stats[:, i] for i in range(4))
    top_p = jnp.max(lse_p, axis=0)
    w_p = jnp.exp(lse_p - top_p)
    total = jnp.sum(w_p, axis=0)
    lz_p = top_p + jnp.log(total)
    top_q = jnp.max(lse_q, axis=0)
    lz_q = top_q + jnp.log(jnp.sum(jnp.exp(lse_q - top_q), axis=0))
    kl_val = jnp.sum(w_p * ratio, axis=0) / total - lz_p + lz_q
    logprobs = jnp.sum(chosen, axis=0) - lz_p
    penalty = -0.05 * mask * kl_val
    rewards = penalty + done * scores
    delta = penalty + known
    local_gae = jnp.sum(products * delta[:, None, :], axis=2)
    fronts = lax.all_to_all(jnp.broadcast_to(local_gae[:, 0][None], (16, 2)), PLANE, 0, 0, tiled=True)
    incoming = jnp.sum(weights * fronts.T, axis=1, keepdims=True)
    gae = local_gae + decay * incoming
    return rewards, mask * gae, mask * (gae + values), logprobs


def solution(mesh):
    fine = Mesh(np.asarray(mesh.devices).reshape(4, 4, 4, 2), ALL)
    placed = (P(None, PLANE, VOCAB),) * 2 + (P(None, ALL),) * 2 + (P(None, PLANE),) * 5
    return jax.shard_map(
        body,
        mesh=fine,
        in_specs=placed,
        out_specs=(P(None, PLANE),) * 4,
        check_vma=False,
    )
```

time: 198 us -> 177 us (0.89)
  waiting for transfers between devices: 90 us -> 64.3 us
  starting transfers between devices: 21 us -> 32.5 us
  Pallas kernels: 54 us -> 48.9 us
  other arithmetic: 12.1 us -> 9.58 us
    all_gather x1, waiting for transfers between devices: 64.5 us -> 0.02 us  [body(): lax.all_gather(jnp.concatenate([both[:, :SHARED].reshape(2 * SHARED, 640)...]
    ppermute x0 -> x12, waiting for transfers between devices: none -> 40.7 us  [the longest x9 25.2 us: near(): return lax.ppermute(value, (axis, 'core'), pairs)]
    ppermute x0 -> x12, starting transfers between devices: none -> 20.5 us  [the longest x9 11.2 us: near(): return lax.ppermute(value, (axis, 'core'), pairs)]
    all_to_all x3 -> x2, starting transfers between devices: 20.2 us -> 9.3 us  [the longest x1 5.84 us: body(): stats = lax.all_to_all(stats, ALL, 0, 0, tiled=True).reshape(128, 4, 2, tok)]
    all_to_all x3 -> x2, waiting for transfers between devices: 23 us -> 16.2 us  [the longest x1 8.79 us: body(): stats = lax.all_to_all(stats, ALL, 0, 0, tiled=True).reshape(128, 4, 2, tok)]
    pallas_call x2, Pallas kernels: 54 us -> 48.9 us  [stats_call(): pl.pallas_call(kernel, in_specs=[pl.BlockSpec(memory_space=space) for spa...]
    ppermute x4 -> x13, waiting for transfers between devices: 2.41 us -> 7.38 us  [swap_cores(): return lax.ppermute(value, 'core', [(0, 1), (1, 0)])]
    unnamed x3 -> x15, local copies, waits for them, and re-layouts: 0.11 us -> 2.36 us
  transfers between devices with their start and end apart: 8 -> 28, of which waited for: 6 -> 17; matrix products, arithmetic and copies ran while one was open for 4% -> 3% of each run, Pallas kernels for 14% -> 11%
where the time goes in v2:
time: 177 us; the launch traced here: 176 us
  waiting for transfers between devices  64.3 us (36%)
  Pallas kernels  48.9 us (28%)
  starting transfers between devices  32.5 us (18%)
  between operations  14.4 us (8%)
  other arithmetic  9.58 us (5%)
  local copies, waits for them, and re-layouts  6.37 us (4%)
    pallas_call x2, Pallas kernels, stats_call(): pl.pallas_call(kernel, in_specs=[pl.BlockSpec(memory_space=space) for spa...  48.9 us
    ppermute x9, waiting for transfers between devices, near(): return lax.ppermute(value, (axis, 'core'), pairs)  25.2 us
    ppermute x3, waiting for transfers between devices, far(): return lax.ppermute(value, (axis, 'core'), pairs)  15.5 us
    ppermute x9, starting transfers between devices, near(): return lax.ppermute(value, (axis, 'core'), pairs)  11.2 us
    ppermute x3, starting transfers between devices, far(): return lax.ppermute(value, (axis, 'core'), pairs)  9.29 us
    all_to_all x1, waiting for transfers between devices, body(): stats = lax.all_to_all(stats, ALL, 0, 0, tiled=True).reshape(128, 4, 2, tok)  8.79 us
    all_to_all x1, waiting for transfers between devices, body(): lax.all_to_all(jnp.broadcast_to(local_gae[:, 0][None], (16, 2)), PLANE, 0...  7.46 us
    ppermute x13, waiting for transfers between devices, swap_cores(): return lax.ppermute(value, 'core', [(0, 1), (1, 0)])  7.38 us
  transfers between devices with their start and end apart: 28, of which 17 were waited for; matrix products, arithmetic and copies ran while one was open for 3% of the time, Pallas kernels for 11%

profile of v2, /device:TPU:0, one launch (start us, length us, event | category | flops | bytes accessed | tf_op | source)
XLA Modules:
  0.0 176.1 jit_solution(5831558622848101103)
XLA Ops:
  7.2 0.7 fusion.25
  8.9 0.8 slice_reduce_fusion.4
  9.8 0.7 shift-right-arithmetic_convert_fusion
  10.8 0.7 pad_maximum_fusion.5
  11.6 0.6 fusion.7
  12.2 0.9 pad_maximum_fusion.4
  13.2 1.3 collective-permute-done
  14.5 0.9 broadcast_select_fusion.8
  15.5 1.6 collective-permute-start.1
  17.2 2.8 %collective-permute-start.3 = (bf16[48,1280]{1,0:T(8,128)(2,1)S(1)}, bf16[48,1280]{1,0:T(8,128)(2,1)S(1)}, u32[]{:S(2)}, u32[]{:S(2)}) collective-permute-start(bf16[48,1280]{1,0:T(8,128)(2,1)S(1)} %fusion.4), channel_id=1, source_target_pairs={{0,4},{1,5},{2,6},{3,7},{4,0},{5,1},{6,2},{7,3},{8,12},{9,13},{10,... | collective-permute-start | bytes 368648 | tf_op jit(solution)/shard_map/ppermute | solution.py:32
  20.0 6.7 %collective-permute-done.3 = bf16[48,1280]{1,0:T(8,128)(2,1)S(1)} collective-permute-done((bf16[48,1280]{1,0:T(8,128)(2,1)S(1)}, bf16[48,1280]{1,0:T(8,128)(2,1)S(1)}, u32[]{:S(2)}, u32[]{:S(2)}) %collective-permute-start.3) | collective-permute-done | bytes 122912 | tf_op jit(solution)/shard_map/ppermute | solution.py:32
  26.7 0.5 collective-permute-start.2
  27.2 0.8 collective-permute-done.4
  28.6 1.6 collective-permute-start.10
  30.3 2.0 %collective-permute-start.5 = (bf16[2,4,24,1280]{3,2,1,0:T(8,128)(2,1)S(1)}, bf16[2,4,24,1280]{3,2,1,0:T(8,128)(2,1)S(1)}, u32[]{:S(2)}, u32[]{:S(2)}) collective-permute-start(bf16[2,4,24,1280]{3,2,1,0:T(8,128)(2,1)S(1)} %get-tuple-element.35), channel_id=1, source_target_pairs={{0,8},{1,25},{8,16},{9,1},{16,24},{17,9},{24,0},{25,17},{2,10},{3,... | collective-permute-start | bytes 1474568 | tf_op jit(solution)/shard_map/ppermute | solution.py:27
  32.3 2.9 %collective-permute-start.12 = (bf16[4,24,1280]{2,1,0:T(8,128)(2,1)S(1)}, bf16[4,24,1280]{2,1,0:T(8,128)(2,1)S(1)}, u32[]{:S(2)}, u32[]{:S(2)}) collective-permute-start(bf16[4,24,1280]{2,1,0:T(8,128)(2,1)S(1)} %get-tuple-element.32), channel_id=1, source_target_pairs={{0,64},{1,65},{32,96},{33,97},{64,0},{65,1},{96,32},{97,33},{2,66}... | collective-permute-start | bytes 737288 | tf_op jit(solution)/shard_map/ppermute | solution.py:32
  35.2 3.6 %collective-permute-start.7 = (bf16[4,24,1280]{2,1,0:T(8,128)(2,1)S(1)}, bf16[4,24,1280]{2,1,0:T(8,128)(2,1)S(1)}, u32[]{:S(2)}, u32[]{:S(2)}) collective-permute-start(bf16[4,24,1280]{2,1,0:T(8,128)(2,1)S(1)} %get-tuple-element.33), channel_id=1, source_target_pairs={{0,16},{1,17},{8,24},{9,25},{16,0},{17,1},{24,8},{25,9},{2,18},{3,... | collective-permute-start | bytes 737288 | tf_op jit(solution)/shard_map/ppermute | solution.py:32
  38.8 6.7 %collective-permute-done.12 = bf16[4,24,1280]{2,1,0:T(8,128)(2,1)S(1)} collective-permute-done((bf16[4,24,1280]{2,1,0:T(8,128)(2,1)S(1)}, bf16[4,24,1280]{2,1,0:T(8,128)(2,1)S(1)}, u32[]{:S(2)}, u32[]{:S(2)}) %collective-permute-start.12) | collective-permute-done | bytes 245792 | tf_op jit(solution)/shard_map/ppermute | solution.py:32
  45.5 0.5 collective-permute-start.11
  46.0 2.1 %collective-permute-done.7 = bf16[4,24,1280]{2,1,0:T(8,128)(2,1)S(1)} collective-permute-done((bf16[4,24,1280]{2,1,0:T(8,128)(2,1)S(1)}, bf16[4,24,1280]{2,1,0:T(8,128)(2,1)S(1)}, u32[]{:S(2)}, u32[]{:S(2)}) %collective-permute-start.7) | collective-permute-done | bytes 245792 | tf_op jit(solution)/shard_map/ppermute | solution.py:32
  48.0 0.5 collective-permute-start.6
  49.1 1.0 collective-permute-start.17
  50.3 0.4 broadcast_select_fusion.1
  50.7 1.6 collective-permute-start.15
  52.3 0.9 copy-done
  53.3 12.8 %collective-permute-done.17.refs_5_ = bf16[2,4,48,1280]{3,2,1,0:T(8,128)(2,1)} collective-permute-done((bf16[2,4,48,1280]{3,2,1,0:T(8,128)(2,1)S(1)}, bf16[2,4,48,1280]{3,2,1,0:T(8,128)(2,1)}, u32[]{:S(2)}, u32[]{:S(2)}) %collective-permute-start.17) | collective-permute-done | bytes 983072 | tf_op jit(solution)/shard_map/ppermute | solution.py:27
  66.0 1.4 collective-permute-done.15.refs_4_
  67.5 1.8 collective-permute-start.14
  69.2 1.6 collective-permute-start.18
  71.0 1.2 copy-done.1
  72.2 19.1 %early_stats.1 = (f32[16,8,128]{2,1,0:T(8,128)S(1)}, f32[384,1152]{1,0:T(8,128)}) custom-call(s32[4]{0:T(128)S(1)} %pad_add_fusion.where_ref, bf16[2,4,48,1280]{3,2,1,0:T(8,128)(2,1)S(1)} %copy-done.1, bf16[2,4,48,1280]{3,2,1,0:T(8,128)(2,1)S(1)} %get-tuple-element.26.refs_1_, bf16[2,4,48,1280]{3,2,1,0:T(8,128)(2,1)S(1)} %get-tuple-element.29.refs_2_, ...), custom_call_target="tpu_custom_call" | custom-call | flops 1 | bytes 1 | tf_op jit(solution)/shard_map/early_stats/pallas_call | solution.py:219
  91.4 0.5 collective-permute-done.14.refs_1_
  91.9 10.5 %collective-permute-done.18.refs_5_ = bf16[2,4,48,1280]{3,2,1,0:T(8,128)(2,1)} collective-permute-done((bf16[2,4,48,1280]{3,2,1,0:T(8,128)(2,1)}, bf16[2,4,48,1280]{3,2,1,0:T(8,128)(2,1)}, u32[]{:S(2)}, u32[]{:S(2)}) %collective-permute-start.18) | collective-permute-done | bytes 983072 | tf_op jit(solution)/shard_map/ppermute | solution.py:27
  102.4 0.5 collective-permute-start.22
  102.9 0.5 collective-permute-start.24
  103.5 0.9 slice_convert_fusion
  104.7 0.4 collective-permute-done.21.refs_2_
  105.2 2.8 %collective-permute-done.22.refs_3_ = bf16[2,4,48,1280]{3,2,1,0:T(8,128)(2,1)S(1)} collective-permute-done((bf16[2,4,48,1280]{3,2,1,0:T(8,128)(2,1)}, bf16[2,4,48,1280]{3,2,1,0:T(8,128)(2,1)S(1)}, u32[]{:S(2)}, u32[]{:S(2)}) %collective-permute-start.22) | collective-permute-done | bytes 983072 | tf_op jit(solution)/shard_map/ppermute | solution.py:22
  108.1 1.4 collective-permute-done.24.refs_7_
  109.5 29.8 %late_stats.1 = f32[16,8,128]{2,1,0:T(8,128)S(1)} custom-call(s32[4]{0:T(128)S(1)} %pad_add_fusion.where_ref, s32[16,64,1]{2,1,0:T(8,128)S(1)} %copy.56.ids_ref, bf16[2,4,48,1280]{3,2,1,0:T(8,128)(2,1)} %collective-permute-done.9.refs_0_, bf16[2,4,48,1280]{3,2,1,0:T(8,128)(2,1)} %collective-permute-done.14.refs_1_, ...), custom_call_target="tpu_custom_call", output_to_operand_aliasing={{}: (14, {})} | custom-call | flops 1 | bytes 1 | tf_op jit(solution)/shard_map/late_stats/pallas_call | solution.py:219
  139.4 0.8 copy.57
  140.2 5.8 %all-to-all-start = ((f32[128,1,256]{2,1,0:T(1,128)}), f32[128,1,256]{2,1,0:T(1,128)S(1)}, u32[]{:S(2)}, u32[]{:S(2)}) async-start(f32[128,1,256]{2,1,0:T(1,128)} %copy.57), calls=%async_computation | async-start | bytes 262144 | tf_op jit(solution)/shard_map/all_to_all | solution.py:383
  146.7 8.8 %all-to-all-done = f32[128,1,256]{2,1,0:T(1,128)S(1)} async-done(((f32[128,1,256]{2,1,0:T(1,128)}), f32[128,1,256]{2,1,0:T(1,128)S(1)}, u32[]{:S(2)}, u32[]{:S(2)}) %all-to-all-start) | async-done | bytes 131104 | tf_op jit(solution)/shard_map/all_to_all | solution.py:383
  155.9 0.6 fusion.23
  156.8 0.6 broadcast_in_dim.134
  157.4 3.5 %all-to-all-start.1 = ((f32[16,1,2]{2,1,0:T(1,128)}), f32[16,1,2]{2,1,0:T(1,128)S(1)}, u32[]{:S(2)}, u32[]{:S(2)}) async-start(f32[16,1,2]{2,1,0:T(1,128)} %broadcast_in_dim.134), calls=%async_computation.1 | async-start | bytes 16384 | tf_op jit(solution)/shard_map/all_to_all | solution.py:397
  161.0 7.5 %all-to-all-done.1 = f32[16,1,2]{2,1,0:T(1,128)S(1)} async-done(((f32[16,1,2]{2,1,0:T(1,128)}), f32[16,1,2]{2,1,0:T(1,128)S(1)}, u32[]{:S(2)}, u32[]{:S(2)}) %all-to-all-start.1) | async-done | bytes 160 | tf_op jit(solution)/shard_map/all_to_all | solution.py:397
  168.6 0.7 add_multiply_fusion
  (104 shorter events, 5.4 us)
Async XLA Ops:
  7.2 96.3 %all-gather.3.cloned.1.call-start = ((), (), s32[]{:S(2)}) async-start(), calls=%async_computation.2 | async-start | bytes 6604800 | tf_op jit(solution)/shard_map/all_gather | solution.py:334
  13.1 1.4 collective-permute-start
  15.5 11.2 %collective-permute-start.1 = (bf16[2,48,1280]{2,1,0:T(8,128)(2,1)S(1)}, bf16[2,48,1280]{2,1,0:T(8,128)(2,1)S(1)}, u32[]{:S(2)}, u32[]{:S(2)}) collective-permute-start(bf16[2,48,1280]{2,1,0:T(8,128)(2,1)S(1)} %get-tuple-element.45), channel_id=1, source_target_pairs={{0,2},{1,7},{2,4},{3,1},{4,6},{5,3},{6,0},{7,5},{8,10},{9,15},{10,... | collective-permute-start | bytes 737288 | tf_op jit(solution)/shard_map/ppermute | solution.py:27
  17.2 9.5 %collective-permute-start.3 = (bf16[48,1280]{1,0:T(8,128)(2,1)S(1)}, bf16[48,1280]{1,0:T(8,128)(2,1)S(1)}, u32[]{:S(2)}, u32[]{:S(2)}) collective-permute-start(bf16[48,1280]{1,0:T(8,128)(2,1)S(1)} %fusion.4), channel_id=1, source_target_pairs={{0,4},{1,5},{2,6},{3,7},{4,0},{5,1},{6,2},{7,3},{8,12},{9,13},{10,... | collective-permute-start | bytes 368648 | tf_op jit(solution)/shard_map/ppermute | solution.py:32
  26.7 1.3 collective-permute-start.4
  26.7 1.7 collective-permute-start.2
  28.6 16.9 %collective-permute-start.10 = (bf16[2,4,24,1280]{3,2,1,0:T(8,128)(2,1)S(1)}, bf16[2,4,24,1280]{3,2,1,0:T(8,128)(2,1)S(1)}, u32[]{:S(2)}, u32[]{:S(2)}) collective-permute-start(bf16[2,4,24,1280]{3,2,1,0:T(8,128)(2,1)S(1)} %get-tuple-element.34), channel_id=1, source_target_pairs={{0,32},{1,97},{32,64},{33,1},{64,96},{65,33},{96,0},{97,65},{2,34}... | collective-permute-start | bytes 1474568 | tf_op jit(solution)/shard_map/ppermute | solution.py:27
  30.3 17.8 %collective-permute-start.5 = (bf16[2,4,24,1280]{3,2,1,0:T(8,128)(2,1)S(1)}, bf16[2,4,24,1280]{3,2,1,0:T(8,128)(2,1)S(1)}, u32[]{:S(2)}, u32[]{:S(2)}) collective-permute-start(bf16[2,4,24,1280]{3,2,1,0:T(8,128)(2,1)S(1)} %get-tuple-element.35), channel_id=1, source_target_pairs={{0,8},{1,25},{8,16},{9,1},{16,24},{17,9},{24,0},{25,17},{2,10},{3,... | collective-permute-start | bytes 1474568 | tf_op jit(solution)/shard_map/ppermute | solution.py:27
  32.3 13.2 %collective-permute-start.12 = (bf16[4,24,1280]{2,1,0:T(8,128)(2,1)S(1)}, bf16[4,24,1280]{2,1,0:T(8,128)(2,1)S(1)}, u32[]{:S(2)}, u32[]{:S(2)}) collective-permute-start(bf16[4,24,1280]{2,1,0:T(8,128)(2,1)S(1)} %get-tuple-element.32), channel_id=1, source_target_pairs={{0,64},{1,65},{32,96},{33,97},{64,0},{65,1},{96,32},{97,33},{2,66}... | collective-permute-start | bytes 737288 | tf_op jit(solution)/shard_map/ppermute | solution.py:32
  35.2 12.9 %collective-permute-start.7 = (bf16[4,24,1280]{2,1,0:T(8,128)(2,1)S(1)}, bf16[4,24,1280]{2,1,0:T(8,128)(2,1)S(1)}, u32[]{:S(2)}, u32[]{:S(2)}) collective-permute-start(bf16[4,24,1280]{2,1,0:T(8,128)(2,1)S(1)} %get-tuple-element.33), channel_id=1, source_target_pairs={{0,16},{1,17},{8,24},{9,25},{16,0},{17,1},{24,8},{25,9},{2,18},{3,... | collective-permute-start | bytes 737288 | tf_op jit(solution)/shard_map/ppermute | solution.py:32
  45.5 3.1 %collective-permute-start.13 = (bf16[4,24,1280]{2,1,0:T(8,128)(2,1)S(1)}, bf16[4,24,1280]{2,1,0:T(8,128)(2,1)S(1)}, u32[]{:S(2)}, u32[]{:S(2)}) collective-permute-start(bf16[4,24,1280]{2,1,0:T(8,128)(2,1)S(1)} %collective-permute-done.12), channel_id=1, source_target_pairs={{0,1},{1,0},{2,3},{3,2},{4,5},{5,4},{6,7},{7,6},{8,9},{9,8},{10,11... | collective-permute-start | bytes 737288 | tf_op jit(solution)/shard_map/ppermute | solution.py:22
  45.5 3.1 %collective-permute-start.11 = (bf16[2,4,24,1280]{3,2,1,0:T(8,128)(2,1)S(1)}, bf16[2,4,24,1280]{3,2,1,0:T(8,128)(2,1)S(1)}, u32[]{:S(2)}, u32[]{:S(2)}) collective-permute-start(bf16[2,4,24,1280]{3,2,1,0:T(8,128)(2,1)S(1)} %collective-permute-done.10), channel_id=1, source_target_pairs={{0,1},{1,0},{2,3},{3,2},{4,5},{5,4},{6,7},{7,6},{8,9},{9,8},{10,11... | collective-permute-start | bytes 1474568 | tf_op jit(solution)/shard_map/ppermute | solution.py:22
  48.0 2.0 %collective-permute-start.8 = (bf16[4,24,1280]{2,1,0:T(8,128)(2,1)S(1)}, bf16[4,24,1280]{2,1,0:T(8,128)(2,1)S(1)}, u32[]{:S(2)}, u32[]{:S(2)}) collective-permute-start(bf16[4,24,1280]{2,1,0:T(8,128)(2,1)S(1)} %collective-permute-done.7), channel_id=1, source_target_pairs={{0,1},{1,0},{2,3},{3,2},{4,5},{5,4},{6,7},{7,6},{8,9},{9,8},{10,11... | collective-permute-start | bytes 737288 | tf_op jit(solution)/shard_map/ppermute | solution.py:22
  48.0 2.2 %collective-permute-start.6 = (bf16[2,4,24,1280]{3,2,1,0:T(8,128)(2,1)S(1)}, bf16[2,4,24,1280]{3,2,1,0:T(8,128)(2,1)S(1)}, u32[]{:S(2)}, u32[]{:S(2)}) collective-permute-start(bf16[2,4,24,1280]{3,2,1,0:T(8,128)(2,1)S(1)} %collective-permute-done.5), channel_id=1, source_target_pairs={{0,1},{1,0},{2,3},{3,2},{4,5},{5,4},{6,7},{7,6},{8,9},{9,8},{10,11... | collective-permute-start | bytes 1474568 | tf_op jit(solution)/shard_map/ppermute | solution.py:22
  49.1 17.0 %collective-permute-start.17 = (bf16[2,4,48,1280]{3,2,1,0:T(8,128)(2,1)S(1)}, bf16[2,4,48,1280]{3,2,1,0:T(8,128)(2,1)}, u32[]{:S(2)}, u32[]{:S(2)}) collective-permute-start(bf16[2,4,48,1280]{3,2,1,0:T(8,128)(2,1)S(1)} %get-tuple-element.26.refs_1_), channel_id=1, source_target_pairs={{0,8},{1,25},{8,16},{9,1},{16,24},{17,9},{24,0},{25,17},{2,10},{3,... | collective-permute-start | bytes 2949128 | tf_op jit(solution)/shard_map/ppermute | solution.py:27
  50.3 20.5 %copy-start.2 = (f32[2,32]{1,0:T(2,128)S(1)}, f32[2,32]{1,0:T(2,128)}, u32[]{:S(2)}) copy-start(f32[2,32]{1,0:T(2,128)} %param.17) | copy-start | bytes 772
  50.7 16.8 %collective-permute-start.15 = (bf16[2,4,48,1280]{3,2,1,0:T(8,128)(2,1)S(1)}, bf16[2,4,48,1280]{3,2,1,0:T(8,128)(2,1)}, u32[]{:S(2)}, u32[]{:S(2)}) collective-permute-start(bf16[2,4,48,1280]{3,2,1,0:T(8,128)(2,1)S(1)} %get-tuple-element.28.refs_0_), channel_id=1, source_target_pairs={{0,32},{1,97},{32,64},{33,1},{64,96},{65,33},{96,0},{97,65},{2,34}... | collective-permute-start | bytes 2949128 | tf_op jit(solution)/shard_map/ppermute | solution.py:27
  52.3 0.9 copy-start
  66.0 4.8 %collective-permute-start.20 = (bf16[2,4,48,1280]{3,2,1,0:T(8,128)(2,1)}, bf16[2,4,48,1280]{3,2,1,0:T(8,128)(2,1)}, u32[]{:S(2)}, u32[]{:S(2)}) collective-permute-start(bf16[2,4,48,1280]{3,2,1,0:T(8,128)(2,1)} %collective-permute-done.17.refs_5_), channel_id=1, source_target_pairs={{0,1},{1,0},{2,3},{3,2},{4,5},{5,4},{6,7},{7,6},{8,9},{9,8},{10,11... | collective-permute-start | bytes 2949128 | tf_op jit(solution)/shard_map/ppermute | solution.py:22
  67.5 3.5 %collective-permute-start.19 = (bf16[2,4,48,1280]{3,2,1,0:T(8,128)(2,1)}, bf16[2,4,48,1280]{3,2,1,0:T(8,128)(2,1)}, u32[]{:S(2)}, u32[]{:S(2)}) collective-permute-start(bf16[2,4,48,1280]{3,2,1,0:T(8,128)(2,1)} %collective-permute-done.15.refs_4_), channel_id=1, source_target_pairs={{0,1},{1,0},{2,3},{3,2},{4,5},{5,4},{6,7},{7,6},{8,9},{9,8},{10,11... | collective-permute-start | bytes 2949128 | tf_op jit(solution)/shard_map/ppermute | solution.py:22
  67.5 24.4 %collective-permute-start.14 = (bf16[2,4,48,1280]{3,2,1,0:T(8,128)(2,1)S(1)}, bf16[2,4,48,1280]{3,2,1,0:T(8,128)(2,1)}, u32[]{:S(2)}, u32[]{:S(2)}) collective-permute-start(bf16[2,4,48,1280]{3,2,1,0:T(8,128)(2,1)S(1)} %get-tuple-element.27.refs_3_), channel_id=1, source_target_pairs={{0,8},{1,25},{8,16},{9,1},{16,24},{17,9},{24,0},{25,17},{2,10},{3,... | collective-permute-start | bytes 2949128 | tf_op jit(solution)/shard_map/ppermute | solution.py:27
  69.2 22.6 %collective-permute-start.9 = (bf16[2,4,48,1280]{3,2,1,0:T(8,128)(2,1)S(1)}, bf16[2,4,48,1280]{3,2,1,0:T(8,128)(2,1)}, u32[]{:S(2)}, u32[]{:S(2)}) collective-permute-start(bf16[2,4,48,1280]{3,2,1,0:T(8,128)(2,1)S(1)} %get-tuple-element.29.refs_2_), channel_id=1, source_target_pairs={{0,32},{1,97},{32,64},{33,1},{64,96},{65,33},{96,0},{97,65},{2,34}... | collective-permute-start | bytes 2949128 | tf_op jit(solution)/shard_map/ppermute | solution.py:27
  69.2 33.1 %collective-permute-start.18 = (bf16[2,4,48,1280]{3,2,1,0:T(8,128)(2,1)}, bf16[2,4,48,1280]{3,2,1,0:T(8,128)(2,1)}, u32[]{:S(2)}, u32[]{:S(2)}) collective-permute-start(bf16[2,4,48,1280]{3,2,1,0:T(8,128)(2,1)} %collective-permute-done.17.refs_5_), channel_id=1, source_target_pairs={{0,8},{1,25},{8,16},{9,1},{16,24},{17,9},{24,0},{25,17},{2,10},{3,... | collective-permute-start | bytes 2949128 | tf_op jit(solution)/shard_map/ppermute | solution.py:27
  70.8 31.5 %collective-permute-start.16 = (bf16[2,4,48,1280]{3,2,1,0:T(8,128)(2,1)}, bf16[2,4,48,1280]{3,2,1,0:T(8,128)(2,1)}, u32[]{:S(2)}, u32[]{:S(2)}) collective-permute-start(bf16[2,4,48,1280]{3,2,1,0:T(8,128)(2,1)} %collective-permute-done.15.refs_4_), channel_id=1, source_target_pairs={{0,32},{1,97},{32,64},{33,1},{64,96},{65,33},{96,0},{97,65},{2,34}... | collective-permute-start | bytes 2949128 | tf_op jit(solution)/shard_map/ppermute | solution.py:27
  71.0 1.2 copy-start.1
  102.4 2.8 %collective-permute-start.21 = (bf16[2,4,48,1280]{3,2,1,0:T(8,128)(2,1)}, bf16[2,4,48,1280]{3,2,1,0:T(8,128)(2,1)S(1)}, u32[]{:S(2)}, u32[]{:S(2)}) collective-permute-start(bf16[2,4,48,1280]{3,2,1,0:T(8,128)(2,1)} %collective-permute-done.9.refs_0_), channel_id=1, source_target_pairs={{0,1},{1,0},{2,3},{3,2},{4,5},{5,4},{6,7},{7,6},{8,9},{9,8},{10,11... | collective-permute-start | bytes 2949128 | tf_op jit(solution)/shard_map/ppermute | solution.py:22
  102.4 5.6 %collective-permute-start.22 = (bf16[2,4,48,1280]{3,2,1,0:T(8,128)(2,1)}, bf16[2,4,48,1280]{3,2,1,0:T(8,128)(2,1)S(1)}, u32[]{:S(2)}, u32[]{:S(2)}) collective-permute-start(bf16[2,4,48,1280]{3,2,1,0:T(8,128)(2,1)} %collective-permute-done.14.refs_1_), channel_id=1, source_target_pairs={{0,1},{1,0},{2,3},{3,2},{4,5},{5,4},{6,7},{7,6},{8,9},{9,8},{10,11... | collective-permute-start | bytes 2949128 | tf_op jit(solution)/shard_map/ppermute | solution.py:22
  102.9 5.2 %collective-permute-start.23 = (bf16[2,4,48,1280]{3,2,1,0:T(8,128)(2,1)}, bf16[2,4,48,1280]{3,2,1,0:T(8,128)(2,1)}, u32[]{:S(2)}, u32[]{:S(2)}) collective-permute-start(bf16[2,4,48,1280]{3,2,1,0:T(8,128)(2,1)} %collective-permute-done.16.refs_4_), channel_id=1, source_target_pairs={{0,1},{1,0},{2,3},{3,2},{4,5},{5,4},{6,7},{7,6},{8,9},{9,8},{10,11... | collective-permute-start | bytes 2949128 | tf_op jit(solution)/shard_map/ppermute | solution.py:22
  102.9 6.6 %collective-permute-start.24 = (bf16[2,4,48,1280]{3,2,1,0:T(8,128)(2,1)}, bf16[2,4,48,1280]{3,2,1,0:T(8,128)(2,1)}, u32[]{:S(2)}, u32[]{:S(2)}) collective-permute-start(bf16[2,4,48,1280]{3,2,1,0:T(8,128)(2,1)} %collective-permute-done.18.refs_5_), channel_id=1, source_target_pairs={{0,1},{1,0},{2,3},{3,2},{4,5},{5,4},{6,7},{7,6},{8,9},{9,8},{10,11... | collective-permute-start | bytes 2949128 | tf_op jit(solution)/shard_map/ppermute | solution.py:22
  109.5 46.4 %copy-start.3 = (s32[2,32]{1,0:T(2,128)S(1)}, s32[2,32]{1,0:T(2,128)}, u32[]{:S(2)}) copy-start(s32[2,32]{1,0:T(2,128)} %param.15) | copy-start | bytes 772
  109.5 46.4 %copy-start.4 = (s32[2,32]{1,0:T(2,128)S(1)}, s32[2,32]{1,0:T(2,128)}, u32[]{:S(2)}) copy-start(s32[2,32]{1,0:T(2,128)} %param.14) | copy-start | bytes 772
  109.5 46.4 %copy-start.5 = (f32[2,32]{1,0:T(2,128)S(1)}, f32[2,32]{1,0:T(2,128)}, u32[]{:S(2)}) copy-start(f32[2,32]{1,0:T(2,128)} %param.16) | copy-start | bytes 772
  140.2 15.2 %all-to-all-start = ((f32[128,1,256]{2,1,0:T(1,128)}), f32[128,1,256]{2,1,0:T(1,128)S(1)}, u32[]{:S(2)}, u32[]{:S(2)}) async-start(f32[128,1,256]{2,1,0:T(1,128)} %copy.57), calls=%async_computation | async-start | bytes 262144 | tf_op jit(solution)/shard_map/all_to_all | solution.py:383
  157.4 11.0 %all-to-all-start.1 = ((f32[16,1,2]{2,1,0:T(1,128)}), f32[16,1,2]{2,1,0:T(1,128)S(1)}, u32[]{:S(2)}, u32[]{:S(2)}) async-start(f32[16,1,2]{2,1,0:T(1,128)} %broadcast_in_dim.134), calls=%async_computation.1 | async-start | bytes 16384 | tf_op jit(solution)/shard_map/all_to_all | solution.py:397
Sparse Core Ops, SparseCore 0:
  12.4 76.7 all-gather.2

commit v3 on v2

v3 whole, which is shorter than its diff:
```python
import functools

import jax
import jax.numpy as jnp
import numpy as np
from jax import lax
from jax.experimental import pallas as pl
from jax.experimental.pallas import tpu as pltpu
from jax.sharding import Mesh, PartitionSpec as P


PLANE = ("y", "z")
VOCAB = ("x", "core")
ALL = PLANE + VOCAB
HALF = 32
STARTS = (0, HALF)
TILE = 256


def swap_cores(value):
    return lax.ppermute(value, "core", [(0, 1), (1, 0)])


def near(value, axis):
    pairs = [(2 * i + c, 2 * ((i + (1, 3)[c]) % 4) + c) for i in range(4) for c in range(2)]
    return lax.ppermute(value, (axis, "core"), pairs)


def far(value, axis):
    pairs = [(2 * i + c, 2 * ((i + 2) % 4) + c) for i in range(4) for c in range(2)]
    return lax.ppermute(value, (axis, "core"), pairs)


def block_products(m, blocks, chunks, head, logits, fresh):
    width = logits.shape[2]
    top = 0
    for count, piece in chunks:
        parts = [piece(m, j) for j in blocks]
        for start in range(0, width, TILE):
            end = min(start + TILE, width)
            product = sum(
                jnp.dot(part, head[j * 1280 : (j + 1) * 1280, start:end], preferred_element_type=jnp.float32)
                for j, part in zip(blocks, parts)
            )
            if fresh:
                logits[m, top : top + count, start:end] = product
            else:
                logits[m, top : top + count, start:end] += product
        top += count


def row_stats(logits, ids, packed):
    chunk = 64
    lane = lax.broadcasted_iota(jnp.int32, (chunk, 128), 1)
    tiles = range(0, logits.shape[2], 128)

    def finish(i, carry):
        here = pl.ds(pl.multiple_of(i * chunk, chunk), chunk)
        top_p = jnp.max(
            functools.reduce(jnp.maximum, [logits[0, here, t : t + 128] for t in tiles]), axis=-1, keepdims=True
        )
        top_q = jnp.max(
            functools.reduce(jnp.maximum, [logits[1, here, t : t + 128] for t in tiles]), axis=-1, keepdims=True
        )
        relative = ids[here, :] - lane
        sums = None
        for t in tiles:
            p, q = logits[0, here, t : t + 128], logits[1, here, t : t + 128]
            expo = jnp.exp(p - top_p)
            terms = expo, expo * (p - q), jnp.exp(q - top_q), jnp.where(relative == t, p, 0.0)
            sums = terms if sums is None else tuple(a + b for a, b in zip(sums, terms))
        sum_p, cross, sum_q, chosen = (jnp.sum(v, axis=-1, keepdims=True) for v in sums)
        found = jnp.where(lane == 0, top_p + jnp.log(sum_p), 0.0)
        found = jnp.where(lane == 1, cross / sum_p, found)
        found = jnp.where(lane == 2, top_q + jnp.log(sum_q), found)
        packed[here, :] = jnp.where(lane == 3, chosen, found)
        return carry

    lax.fori_loop(0, logits.shape[1] // chunk, finish, 0)


def near_blocks(where_ref):
    x = where_ref[2]
    return [lax.rem(x + d, 4) for d in (0, 3, 1, 2)]


def placed_blocks(places, where_ref):
    y, z, core = where_ref[0], where_ref[1], where_ref[3]
    blocks = []
    for kind, by_core in places:
        for (along_0, across_0), (along_1, across_1) in zip(*by_core):
            along = jnp.where(core == 0, along_0, along_1)
            across = jnp.where(core == 0, across_0, across_1)
            dy, dz = (along, across) if kind == 0 else (across, along)
            ctx = lax.rem(y + dy, 4) * 4 + lax.rem(z + dz, 4)
            blocks.append((ctx, STARTS[kind]))
    return blocks


def moved_chunks(refs):
    def chunk(some):
        return 2 * HALF * len(some), lambda m, j: jnp.concatenate([ref[m, j] for ref in some], axis=0)

    return [chunk(refs[i : i + 4]) for i in range(0, len(refs), 4)]


def take_ids(blocks, ids_ref, ids):
    for i, (ctx, start) in enumerate(blocks):
        ids[i * HALF : (i + 1) * HALF, :] = ids_ref[ctx, start : start + HALF, :]


def give_stats(blocks, found, out_ref):
    for i, (ctx, start) in enumerate(blocks):
        out_ref[ctx, :, start : start + HALF] = found[:, i * HALF : (i + 1) * HALF]


class HeadBlocks:
    ahead = 4

    def __init__(self, heads, near_to, buffer, sems):
        self.order = [(m, j) for m in range(2) for j in range(4)]
        self.copies = [
            pltpu.make_async_copy(
                heads[m].at[pl.ds(pl.multiple_of(near_to[j] * 1280, 1280), 1280)],
                buffer[m].at[pl.ds(j * 1280, 1280)] if isinstance(buffer, tuple) else buffer.at[m, pl.ds(j * 1280, 1280)],
                sems.at[m, j],
            )
            for m, j in self.order
        ]
        for copy in self.copies[: self.ahead]:
            copy.start()

    def wait(self, k):
        self.copies[k].wait()
        if k + self.ahead < len(self.copies):
            self.copies[k + self.ahead].start()


def early_kernel(places, where_ref, ids_ref, *refs):
    count = len(places)
    sources, heads = refs[:count], refs[count : count + 2]
    out_ref, packed, logits, ids, sems, buffer, moved, moved_sems = refs[count + 2 :]
    inputs = [
        [pltpu.make_async_copy(sources[k].at[m], moved.at[k, m], moved_sems.at[k, m]) for k in range(count)]
        for m in range(2)
    ]
    for copy in inputs[0]:
        copy.start()
    stream = HeadBlocks(heads, near_blocks(where_ref), buffer, sems)
    for copy in inputs[1]:
        copy.start()
    blocks = placed_blocks(places, where_ref)
    take_ids(blocks, ids_ref, ids)
    chunks = moved_chunks([moved.at[k] for k in range(count)])
    for m, groups in enumerate((((0,), (1,), (2, 3)), ((0, 1), (2, 3)))):
        for copy in inputs[m]:
            copy.wait()
        for group in groups:
            for j in group:
                stream.wait(4 * m + j)
            block_products(m, group, chunks, buffer.at[m], logits, group[0] == 0)
    row_stats(logits, ids, packed)
    give_stats(blocks, packed[...].T[0:8], out_ref)


def late_kernel(places, where_ref, ids_ref, *refs):
    count = len(places)
    moved, heads = refs[:count], refs[count : count + 2]
    out_ref, head_p, head_q, packed, logits, ids, sems = refs[count + 3 :]
    buffer = (head_p, head_q)
    stream = HeadBlocks(heads, near_blocks(where_ref), buffer, sems)
    blocks = placed_blocks(places, where_ref)
    take_ids(blocks, ids_ref, ids)
    chunks = moved_chunks(moved)
    for m, groups in enumerate((((0,), (1,), (2, 3)), ((0, 1), (2,), (3,)))):
        for group in groups:
            for j in group:
                stream.wait(4 * m + j)
            block_products(m, group, chunks, buffer[m], logits, group[0] == 0)
    row_stats(logits, ids, packed)
    give_stats(blocks, packed[...].T[0:8], out_ref)


def last_kernel(places, where_ref, ids_ref, *refs):
    count = len(places)
    moved, heads = refs[:count], refs[count : count + 2]
    out_ref, packed, logits, ids, sems = refs[count + 3 :]
    blocks = placed_blocks(places, where_ref)
    take_ids(blocks, ids_ref, ids)
    chunks = moved_chunks(moved)
    for m in range(2):
        block_products(m, range(4), chunks, heads[m], logits, True)
    row_stats(logits, ids, packed)
    give_stats(blocks, packed[...].T[0:8], out_ref)


def stats_call(kernel, name, where, ids, pieces, heads, before, limit):
    vmem, hbm = pl.BlockSpec(memory_space=pltpu.VMEM), pl.BlockSpec(memory_space=pltpu.HBM)
    depth, width = heads[0].shape
    count = len(pieces)
    rows = 2 * HALF * count
    chain = () if before is None else (before,)
    operands = (where, ids, *[a for a, _ in pieces], *heads, *chain)
    early, late = kernel is early_kernel, kernel is late_kernel
    outs = [jax.ShapeDtypeStruct((16, 8, 128), jnp.float32)]
    if late:
        outs += [jax.ShapeDtypeStruct(h.shape, h.dtype) for h in heads]
    scratch = [
        pltpu.VMEM((rows, 128), jnp.float32),
        pltpu.VMEM((2, rows, width), jnp.float32),
        pltpu.VMEM((rows, 1), jnp.int32),
        pltpu.SemaphoreType.DMA((2, 4)),
    ]
    if early:
        scratch += [
            pltpu.VMEM((2, depth, width), jnp.bfloat16),
            pltpu.VMEM((count, 2, 4, 2 * HALF, 1280), jnp.bfloat16),
            pltpu.SemaphoreType.DMA((count, 2)),
        ]
    return pl.pallas_call(
        functools.partial(kernel, tuple(p for _, p in pieces)),
        in_specs=[pl.BlockSpec(memory_space=pltpu.SMEM), vmem]
        + [hbm if early else vmem] * count
        + [hbm if early or late else vmem] * 2
        + [vmem] * len(chain),
        out_specs=[vmem] * len(outs),
        out_shape=outs,
        scratch_shapes=scratch,
        input_output_aliases={len(operands) - 1: 0} if chain else {},
        compiler_params=pltpu.CompilerParams(vmem_limit_bytes=limit << 20),
        cost_estimate=pl.CostEstimate(
            flops=4 * rows * depth * width,
            bytes_accessed=4 * depth * (rows + width),
            transcendentals=2 * rows * width,
        ),
        name=name,
    )(*operands)


def chain_products(coef):
    count = coef.shape[1]
    t = lax.broadcasted_iota(jnp.int32, (1, count, count), 1)
    u = lax.broadcasted_iota(jnp.int32, (1, count, count), 2)
    before = jnp.concatenate([jnp.ones_like(coef[:, :1]), coef[:, :-1]], axis=1)
    factors = jnp.where(u > t, before[:, None, :], 1.0)
    shift = 1
    while shift < count:
        moved = jnp.pad(factors[:, :, :-shift], ((0, 0), (0, 0), (shift, 0)), constant_values=1.0)
        factors = factors * moved
        shift *= 2
    return jnp.where(u >= t, factors, 0.0)


def gather_line(first, value, axis):
    beside, across = near(value, axis), far(jnp.where(first, value[0], value[1]), axis)
    beside_2, across_2 = swap_cores(beside), swap_cores(across)
    before = jnp.where(first, beside, beside_2)
    after = jnp.where(first, beside_2, beside)
    opposite = jnp.stack([jnp.where(first, across, across_2), jnp.where(first, across_2, across)])
    return value, before, after, opposite


def body(hidden_policy, hidden_ref, head_policy, head_ref, token_ids, response_mask, done_flags, scores, values):
    y, z, x, core = (lax.axis_index(a) for a in ALL)
    width = head_policy.shape[1]
    tok = token_ids.shape[1]
    ctx = y * 4 + z
    first = core == 0
    where = jnp.stack([y, z, x, core])
    heads = (head_policy, head_ref)

    both = jnp.stack([hidden_policy.reshape(64, 640), hidden_ref.reshape(64, 640)])
    got = swap_cores(both)
    rest = jnp.concatenate([jnp.where(first, both, got), jnp.where(first, got, both)], axis=-1)

    mask = response_mask.astype(jnp.float32)
    done = done_flags.astype(jnp.float32)
    coef = 0.998 * (1.0 - done)
    products = chain_products(coef)
    decay = products[:, :, -1] * coef[:, -1:]

    line = jnp.stack(gather_line(first, rest, "x"), axis=1)
    shared = jnp.concatenate(
        [token_ids.astype(jnp.float32), decay[:, :1], values[:, :1], jnp.zeros((2, 30), jnp.float32)], axis=1
    )
    shared, line = lax.optimization_barrier((shared, line))
    shared = lax.all_to_all(jnp.broadcast_to(shared.reshape(1, 128), (16, 128)), PLANE, 0, 0, tiled=True)
    shared = shared.reshape(16, 2, 64)
    columns = (ctx * 8 + x * 2 + core) * width
    ids = shared[:, :, :tok].reshape(16, 64, 1).astype(jnp.int32) - columns
    head_decay, first_value = shared[:, :, tok].T, shared[:, :, tok + 1].T

    arrays = []
    for kind, (axis_2, axis_3) in enumerate((("z", "y"), ("y", "z"))):
        own, before, after, opposite = gather_line(first, line[:, :, kind * HALF : (kind + 1) * HALF], axis_2)
        own, before, after, opposite, ids = lax.optimization_barrier((own, before, after, opposite, ids))
        lower = jnp.concatenate([own, before], axis=2)
        upper = jnp.concatenate([after, opposite], axis=2)
        arrays.append((jnp.where(first, lower, upper), jnp.where(first, upper, lower), axis_3))

    place = lax.broadcasted_iota(jnp.int32, (1, 16), 1)
    following = jnp.sum(jnp.where(place == ctx + 1, first_value, 0.0), axis=1, keepdims=True)
    next_value = jnp.concatenate([values[:, 1:], following], axis=1)
    known = done * scores + (1.0 - done) * next_value - values
    later = chain_products(head_decay)
    weights = jnp.sum(jnp.where(lax.broadcasted_iota(jnp.int32, (1, 16, 1), 1) == ctx + 1, later, 0.0), axis=1)

    def place_of(kind, along, halves):
        across = (0, 3, 1, 2)
        return kind, tuple(
            tuple((along[c], s) for s in across[2 * halves[c] : 2 * halves[c] + 2]) for c in range(2)
        )

    ones, twos, axes = zip(*arrays)
    kinds = range(2)
    ones_1 = [near(ones[k], axes[k]) for k in kinds]
    twos_1 = [near(twos[k], axes[k]) for k in kinds]
    ones_2 = [near(ones_1[k], axes[k]) for k in kinds]
    others_1 = [swap_cores(ones_1[k]) for k in kinds]
    early = [(ones[k], place_of(k, (0, 0), (0, 1))) for k in kinds]
    early += [(twos[k], place_of(k, (0, 0), (1, 0))) for k in kinds]
    early += [(ones_1[k], place_of(k, (3, 1), (0, 1))) for k in kinds]
    early += [(others_1[k], place_of(k, (1, 3), (1, 0))) for k in kinds]
    (stats,) = stats_call(early_kernel, "early_stats", where, ids, early, heads, None, 54)
    *arrived, stats = lax.optimization_barrier((*twos_1, *ones_2, stats))
    twos_1, ones_2 = arrived[:2], arrived[2:]
    late = [(twos_1[k], place_of(k, (3, 1), (1, 0))) for k in kinds]
    late += [(ones_2[k], place_of(k, (2, 2), (0, 1))) for k in kinds]
    last = [(swap_cores(twos_1[k]), place_of(k, (1, 3), (0, 1))) for k in kinds]
    last += [(swap_cores(ones_2[k]), place_of(k, (2, 2), (1, 0))) for k in kinds]
    stats, *heads = stats_call(late_kernel, "late_stats", where, ids, late, heads, stats, 24)
    (stats,) = stats_call(last_kernel, "last_stats", where, ids, last, heads, stats, 24)

    stats = jnp.broadcast_to(stats[:, :4, :64].reshape(16, 1, 256), (16, 8, 256)).reshape(128, 256)
    stats = lax.all_to_all(stats, ALL, 0, 0, tiled=True).reshape(128, 4, 2, tok)
    lse_p, ratio, lse_q, chosen = (stats[:, i] for i in range(4))
    top_p = jnp.max(lse_p, axis=0)
    w_p = jnp.exp(lse_p - top_p)
    total = jnp.sum(w_p, axis=0)
    lz_p = top_p + jnp.log(total)
    top_q = jnp.max(lse_q, axis=0)
    lz_q = top_q + jnp.log(jnp.sum(jnp.exp(lse_q - top_q), axis=0))
    kl_val = jnp.sum(w_p * ratio, axis=0) / total - lz_p + lz_q
    logprobs = jnp.sum(chosen, axis=0) - lz_p
    penalty = -0.05 * mask * kl_val
    rewards = penalty + done * scores
    delta = penalty + known
    local_gae = jnp.sum(products * delta[:, None, :], axis=2)
    fronts = lax.all_to_all(jnp.broadcast_to(local_gae[:, 0][None], (16, 2)), PLANE, 0, 0, tiled=True)
    incoming = jnp.sum(weights * fronts.T, axis=1, keepdims=True)
    gae = local_gae + decay * incoming
    return rewards, mask * gae, mask * (gae + values), logprobs


def solution(mesh):
    fine = Mesh(np.asarray(mesh.devices).reshape(4, 4, 4, 2), ALL)
    placed = (P(None, PLANE, VOCAB),) * 2 + (P(None, ALL),) * 2 + (P(None, PLANE),) * 5
    return jax.shard_map(
        body,
        mesh=fine,
        in_specs=placed,
        out_specs=(P(None, PLANE),) * 4,
        check_vma=False,
    )
```

time: 177 us -> 163 us (0.921)
  between operations: 14.4 us -> 1.2 us
  waiting for transfers between devices: 64.3 us -> 58.5 us
  starting transfers between devices: 32.5 us -> 36.9 us
    ppermute x3, waiting for transfers between devices: 15.5 us -> 6.35 us  [far(): return lax.ppermute(value, (axis, 'core'), pairs)]
    ppermute x9, waiting for transfers between devices: 25.2 us -> 30.9 us  [near(): return lax.ppermute(value, (axis, 'core'), pairs)]
    all_to_all x0 -> x1, starting transfers between devices: none -> 5.03 us  [body(): lax.all_to_all(jnp.broadcast_to(shared.reshape(1, 128), (16, 128)), PLANE...]
    ppermute x13, waiting for transfers between devices: 7.38 us -> 3.21 us  [swap_cores(): return lax.ppermute(value, 'core', [(0, 1), (1, 0)])]
    another operation x3 -> x5, other arithmetic: 0.09 us -> 2.19 us  [gather_line(): jnp.stack([jnp.where(first, across, across_2), jnp.where(first, across_2,...]
    all_to_all x0 -> x1, waiting for transfers between devices: none -> 1.98 us  [body(): lax.all_to_all(jnp.broadcast_to(shared.reshape(1, 128), (16, 128)), PLANE...]
    pallas_call x2 -> x3, Pallas kernels: 48.9 us -> 48.7 us  [stats_call(): pl.pallas_call(functools.partial(kernel, tuple((p for _, p in pieces))),...]
  transfers between devices with their start and end apart: 28 -> 28, of which waited for: 17 -> 14; matrix products, arithmetic and copies ran while one was open for 3% -> 6% of each run, Pallas kernels for 11% -> 23%
where the time goes in v3:
time: 163 us; the launch traced here: 162 us
  waiting for transfers between devices  58.5 us (36%)
  Pallas kernels  48.7 us (30%)
  starting transfers between devices  36.9 us (23%)
  other arithmetic  10.4 us (6%)
  local copies, waits for them, and re-layouts  6.55 us (4%)
    pallas_call x3, Pallas kernels, stats_call(): pl.pallas_call(functools.partial(kernel, tuple((p for _, p in pieces))),...  48.7 us
    ppermute x9, waiting for transfers between devices, near(): return lax.ppermute(value, (axis, 'core'), pairs)  30.9 us
    ppermute x3, starting transfers between devices, far(): return lax.ppermute(value, (axis, 'core'), pairs)  10.7 us
    ppermute x9, starting transfers between devices, near(): return lax.ppermute(value, (axis, 'core'), pairs)  10.2 us
    all_to_all x1, waiting for transfers between devices, body(): stats = lax.all_to_all(stats, ALL, 0, 0, tiled=True).reshape(128, 4, 2, tok)  9.09 us
    all_to_all x1, waiting for transfers between devices, body(): lax.all_to_all(jnp.broadcast_to(local_gae[:, 0][None], (16, 2)), PLANE, 0...  6.99 us
    ppermute x3, waiting for transfers between devices, far(): return lax.ppermute(value, (axis, 'core'), pairs)  6.35 us
    all_to_all x1, starting transfers between devices, body(): stats = lax.all_to_all(stats, ALL, 0, 0, tiled=True).reshape(128, 4, 2, tok)  6.23 us
  transfers between devices with their start and end apart: 28, of which 14 were waited for; matrix products, arithmetic and copies ran while one was open for 6% of the time, Pallas kernels for 23%

profile of v3, /device:TPU:0, one launch (start us, length us, event | category | flops | bytes accessed | tf_op | source)
XLA Modules:
  0.0 162.3 jit_solution(7785823518144934565)
XLA Ops:
  0.6 0.9 pad_maximum_fusion.4
  1.7 0.7 fusion.17
  3.2 1.0 broadcast_select_fusion.8
  4.3 3.2 %collective-permute-start.3 = (bf16[64,1280]{1,0:T(8,128)(2,1)S(1)}, bf16[64,1280]{1,0:T(8,128)(2,1)S(1)}, u32[]{:S(2)}, u32[]{:S(2)}) collective-permute-start(bf16[64,1280]{1,0:T(8,128)(2,1)S(1)} %fusion.2), channel_id=1, source_target_pairs={{0,4},{1,5},{2,6},{3,7},{4,0},{5,1},{6,2},{7,3},{8,12},{9,13},{10,... | collective-permute-start | bytes 491528 | tf_op jit(solution)/shard_map/ppermute | solution.py:31
  7.5 0.6 collective-permute-start.1
  8.2 4.3 %collective-permute-done.3 = bf16[64,1280]{1,0:T(8,128)(2,1)S(1)} collective-permute-done((bf16[64,1280]{1,0:T(8,128)(2,1)S(1)}, bf16[64,1280]{1,0:T(8,128)(2,1)S(1)}, u32[]{:S(2)}, u32[]{:S(2)}) %collective-permute-start.3) | collective-permute-done | bytes 163872 | tf_op jit(solution)/shard_map/ppermute | solution.py:31
  12.5 3.4 %collective-permute-done.1 = bf16[2,64,1280]{2,1,0:T(8,128)(2,1)S(1)} collective-permute-done((bf16[2,64,1280]{2,1,0:T(8,128)(2,1)S(1)}, bf16[2,64,1280]{2,1,0:T(8,128)(2,1)S(1)}, u32[]{:S(2)}, u32[]{:S(2)}) %collective-permute-start.1) | collective-permute-done | bytes 327712 | tf_op jit(solution)/shard_map/ppermute | solution.py:26
  16.1 1.4 collective-permute-done.2
  17.9 4.0 %collective-permute-start.11 = (bf16[4,32,1280]{2,1,0:T(8,128)(2,1)S(1)}, bf16[4,32,1280]{2,1,0:T(8,128)(2,1)S(1)}, u32[]{:S(2)}, u32[]{:S(2)}) collective-permute-start(bf16[4,32,1280]{2,1,0:T(8,128)(2,1)S(1)} %get-tuple-element.56), channel_id=1, source_target_pairs={{0,16},{1,17},{8,24},{9,25},{16,0},{17,1},{24,8},{25,9},{2,18},{3,... | collective-permute-start | bytes 983048 | tf_op jit(solution)/shard_map/ppermute | solution.py:31
  22.0 0.6 broadcast_in_dim.126
  22.6 5.0 %all-to-all-start = ((f32[16,1,128]{2,1,0:T(1,128)}), f32[16,1,128]{2,1,0:T(1,128)S(1)}, u32[]{:S(2)}, u32[]{:S(2)}) async-start(f32[16,1,128]{2,1,0:T(1,128)} %broadcast_in_dim.126), calls=%async_computation | async-start | bytes 16384 | tf_op jit(solution)/shard_map/all_to_all | solution.py:287
  27.6 3.4 %collective-permute-start.7 = (bf16[4,32,1280]{2,1,0:T(8,128)(2,1)S(1)}, bf16[4,32,1280]{2,1,0:T(8,128)(2,1)}, u32[]{:S(2)}, u32[]{:S(2)}) collective-permute-start(bf16[4,32,1280]{2,1,0:T(8,128)(2,1)S(1)} %get-tuple-element.57), channel_id=1, source_target_pairs={{0,64},{1,65},{32,96},{33,97},{64,0},{65,1},{96,32},{97,33},{2,66}... | collective-permute-start | bytes 983048 | tf_op jit(solution)/shard_map/ppermute | solution.py:31
  31.2 1.5 collective-permute-start.9
  32.7 0.6 collective-permute-start.5
  33.3 2.0 %all-to-all-done = f32[16,1,128]{2,1,0:T(1,128)S(1)} async-done(((f32[16,1,128]{2,1,0:T(1,128)}), f32[16,1,128]{2,1,0:T(1,128)S(1)}, u32[]{:S(2)}, u32[]{:S(2)}) %all-to-all-start) | async-done | bytes 8224 | tf_op jit(solution)/shard_map/all_to_all | solution.py:287
  35.3 0.5 broadcast.76
  35.8 0.7 reduce.11
  36.6 2.1 %collective-permute-done.7 = bf16[4,32,1280]{2,1,0:T(8,128)(2,1)} collective-permute-done((bf16[4,32,1280]{2,1,0:T(8,128)(2,1)S(1)}, bf16[4,32,1280]{2,1,0:T(8,128)(2,1)}, u32[]{:S(2)}, u32[]{:S(2)}) %collective-permute-start.7) | collective-permute-done | bytes 327712 | tf_op jit(solution)/shard_map/ppermute | solution.py:31
  38.7 1.0 select_bitcast_fusion.1
  39.8 3.2 %collective-permute-done.9 = bf16[2,4,32,1280]{3,2,1,0:T(8,128)(2,1)S(1)} collective-permute-done((bf16[2,4,32,1280]{3,2,1,0:T(8,128)(2,1)S(1)}, bf16[2,4,32,1280]{3,2,1,0:T(8,128)(2,1)S(1)}, u32[]{:S(2)}, u32[]{:S(2)}) %collective-permute-start.9) | collective-permute-done | bytes 655392 | tf_op jit(solution)/shard_map/ppermute | solution.py:26
  43.1 1.0 select_bitcast_fusion.4
  44.1 1.5 collective-permute-done.5
  45.9 1.7 %collective-permute-done.6 = bf16[2,4,32,1280]{3,2,1,0:T(8,128)(2,1)S(1)} collective-permute-done((bf16[2,4,32,1280]{3,2,1,0:T(8,128)(2,1)S(1)}, bf16[2,4,32,1280]{3,2,1,0:T(8,128)(2,1)S(1)}, u32[]{:S(2)}, u32[]{:S(2)}) %collective-permute-start.6) | collective-permute-done | bytes 655392 | tf_op jit(solution)/shard_map/ppermute | solution.py:21
  48.2 1.6 collective-permute-start.17
  50.2 1.5 collective-permute-start.15
  51.7 15.5 %collective-permute-done.17.refs_5_ = bf16[2,4,64,1280]{3,2,1,0:T(8,128)(2,1)} collective-permute-done((bf16[2,4,64,1280]{3,2,1,0:T(8,128)(2,1)S(1)}, bf16[2,4,64,1280]{3,2,1,0:T(8,128)(2,1)}, u32[]{:S(2)}, u32[]{:S(2)}) %collective-permute-start.17) | collective-permute-done | bytes 1310752 | tf_op jit(solution)/shard_map/ppermute | solution.py:26
  67.2 2.0 %collective-permute-done.15.refs_4_ = bf16[2,4,64,1280]{3,2,1,0:T(8,128)(2,1)} collective-permute-done((bf16[2,4,64,1280]{3,2,1,0:T(8,128)(2,1)S(1)}, bf16[2,4,64,1280]{3,2,1,0:T(8,128)(2,1)}, u32[]{:S(2)}, u32[]{:S(2)}) %collective-permute-start.15) | collective-permute-done | bytes 1310752 | tf_op jit(solution)/shard_map/ppermute | solution.py:26
  69.2 0.6 pad_add_fusion.where_ref
  69.8 1.5 collective-permute-start.14
  71.6 1.2 collective-permute-start.18
  72.8 1.4 collective-permute-start.16
  74.5 1.1 copy.67.ids_ref
  75.6 23.4 %early_stats.1.refs_6_ = f32[16,8,128]{2,1,0:T(8,128)} custom-call(s32[4]{0:T(128)} %pad_add_fusion.where_ref, s32[16,64,1]{2,1,0:T(8,128)} %copy.67.ids_ref, bf16[2,4,64,1280]{3,2,1,0:T(8,128)(2,1)} %copy-done.6, bf16[2,4,64,1280]{3,2,1,0:T(8,128)(2,1)} %copy-done.4, bf16[2,4,64,1280]{3,2,1,0:T(8,128)(2,1)} %copy-done.5, ...), custom_call_target="tpu_custom_call" | custom-call | flops 12079595520 | bytes 34078720 | tf_op jit(solution)/shard_map/early_stats/pallas_call | solution.py:220
  99.0 3.9 %collective-permute-done.18.refs_3_ = bf16[2,4,64,1280]{3,2,1,0:T(8,128)(2,1)} collective-permute-done((bf16[2,4,64,1280]{3,2,1,0:T(8,128)(2,1)}, bf16[2,4,64,1280]{3,2,1,0:T(8,128)(2,1)}, u32[]{:S(2)}, u32[]{:S(2)}) %collective-permute-start.18) | collective-permute-done | bytes 1310752 | tf_op jit(solution)/shard_map/ppermute | solution.py:26
  102.9 1.5 collective-permute-done.16.refs_2_
  104.9 0.5 collective-permute-start.24
  105.7 0.8 copy-done.1
  106.6 14.3 %late_stats.1 = (f32[16,8,128]{2,1,0:T(8,128)S(1)}, bf16[5120,1152]{1,0:T(8,128)(2,1)S(1)}, bf16[5120,1152]{1,0:T(8,128)(2,1)S(1)}) custom-call(s32[4]{0:T(128)S(1)} %copy-done.2, s32[16,64,1]{2,1,0:T(8,128)S(1)} %copy-done, bf16[2,4,64,1280]{3,2,1,0:T(8,128)(2,1)} %collective-permute-done.13.refs_0_, ...), custom_call_target="tpu_custom_call", output_to_operand_aliasing={{0}: (8, {})} | custom-call | flops 6039797760 | bytes 28835840 | tf_op jit(solution)/shard_map/late_stats/pallas_call | solution.py:220
  120.9 11.0 %last_stats.1 = f32[16,8,128]{2,1,0:T(8,128)S(1)} custom-call(s32[4]{0:T(128)S(1)} %copy-done.2, s32[16,64,1]{2,1,0:T(8,128)S(1)} %copy-done, bf16[2,4,64,1280]{3,2,1,0:T(8,128)(2,1)} %collective-permute-done.21.refs_0_, bf16[2,4,64,1280]{3,2,1,0:T(8,128)(2,1)} %collective-permute-done.22.refs_1_, ...), custom_call_target="tpu_custom_call", output_to_operand_aliasing={{}: (8, {})} | custom-call | flops 6039797760 | bytes 28835840 | tf_op jit(solution)/shard_map/last_stats/pallas_call | solution.py:220
  132.1 0.8 copy.68
  132.9 6.2 %all-to-all-start.1 = ((f32[128,1,256]{2,1,0:T(1,128)}), f32[128,1,256]{2,1,0:T(1,128)S(1)}, u32[]{:S(2)}, u32[]{:S(2)}) async-start(f32[128,1,256]{2,1,0:T(1,128)} %copy.68), calls=%async_computation.1 | async-start | bytes 262144 | tf_op jit(solution)/shard_map/all_to_all | solution.py:335
  139.4 9.1 %all-to-all-done.1 = f32[128,1,256]{2,1,0:T(1,128)S(1)} async-done(((f32[128,1,256]{2,1,0:T(1,128)}), f32[128,1,256]{2,1,0:T(1,128)S(1)}, u32[]{:S(2)}, u32[]{:S(2)}) %all-to-all-start.1) | async-done | bytes 131104 | tf_op jit(solution)/shard_map/all_to_all | solution.py:335
  148.9 0.6 fusion.14
  149.8 0.6 broadcast_in_dim.139
  150.4 3.5 %all-to-all-start.2 = ((f32[16,1,2]{2,1,0:T(1,128)}), f32[16,1,2]{2,1,0:T(1,128)S(1)}, u32[]{:S(2)}, u32[]{:S(2)}) async-start(f32[16,1,2]{2,1,0:T(1,128)} %broadcast_in_dim.139), calls=%async_computation.2 | async-start | bytes 16384 | tf_op jit(solution)/shard_map/all_to_all | solution.py:349
  153.9 0.6 fusion.18
  154.5 7.0 %all-to-all-done.2 = f32[16,1,2]{2,1,0:T(1,128)S(1)} async-done(((f32[16,1,2]{2,1,0:T(1,128)}), f32[16,1,2]{2,1,0:T(1,128)S(1)}, u32[]{:S(2)}, u32[]{:S(2)}) %all-to-all-start.2) | async-done | bytes 160 | tf_op jit(solution)/shard_map/all_to_all | solution.py:349
  161.6 0.6 add_multiply_fusion
  (121 shorter events, 6.0 us)
Async XLA Ops:
  1.6 1.6 collective-permute-start
  2.7 5.4 %copy-start.11 = (s32[2,32]{1,0:T(2,128)S(1)}, s32[2,32]{1,0:T(2,128)}, u32[]{:S(2)}) copy-start(s32[2,32]{1,0:T(2,128)} %param.13) | copy-start | bytes 772
  2.9 9.6 %copy-start.7 = (f32[2,32]{1,0:T(2,128)S(1)}, f32[2,32]{1,0:T(2,128)}, u32[]{:S(2)}) copy-start(f32[2,32]{1,0:T(2,128)} %param.17) | copy-start | bytes 772
  4.3 8.2 %collective-permute-start.3 = (bf16[64,1280]{1,0:T(8,128)(2,1)S(1)}, bf16[64,1280]{1,0:T(8,128)(2,1)S(1)}, u32[]{:S(2)}, u32[]{:S(2)}) collective-permute-start(bf16[64,1280]{1,0:T(8,128)(2,1)S(1)} %fusion.2), channel_id=1, source_target_pairs={{0,4},{1,5},{2,6},{3,7},{4,0},{5,1},{6,2},{7,3},{8,12},{9,13},{10,... | collective-permute-start | bytes 491528 | tf_op jit(solution)/shard_map/ppermute | solution.py:31
  7.5 8.5 %collective-permute-start.1 = (bf16[2,64,1280]{2,1,0:T(8,128)(2,1)S(1)}, bf16[2,64,1280]{2,1,0:T(8,128)(2,1)S(1)}, u32[]{:S(2)}, u32[]{:S(2)}) collective-permute-start(bf16[2,64,1280]{2,1,0:T(8,128)(2,1)S(1)} %get-tuple-element.71), channel_id=1, source_target_pairs={{0,2},{1,7},{2,4},{3,1},{4,6},{5,3},{6,0},{7,5},{8,10},{9,15},{10,... | collective-permute-start | bytes 983048 | tf_op jit(solution)/shard_map/ppermute | solution.py:26
  12.5 3.6 %collective-permute-start.4 = (bf16[64,1280]{1,0:T(8,128)(2,1)S(1)}, bf16[64,1280]{1,0:T(8,128)(2,1)S(1)}, u32[]{:S(2)}, u32[]{:S(2)}) collective-permute-start(bf16[64,1280]{1,0:T(8,128)(2,1)S(1)} %collective-permute-done.3), channel_id=1, source_target_pairs={{0,1},{1,0},{2,3},{3,2},{4,5},{5,4},{6,7},{7,6},{8,9},{9,8},{10,11... | collective-permute-start | bytes 491528 | tf_op jit(solution)/shard_map/ppermute | solution.py:21
  16.0 1.6 %collective-permute-start.2 = (bf16[2,64,1280]{2,1,0:T(8,128)(2,1)S(1)}, bf16[2,64,1280]{2,1,0:T(8,128)(2,1)S(1)}, u32[]{:S(2)}, u32[]{:S(2)}) collective-permute-start(bf16[2,64,1280]{2,1,0:T(8,128)(2,1)S(1)} %collective-permute-done.1), channel_id=1, source_target_pairs={{0,1},{1,0},{2,3},{3,2},{4,5},{5,4},{6,7},{7,6},{8,9},{9,8},{10,11... | collective-permute-start | bytes 983048 | tf_op jit(solution)/shard_map/ppermute | solution.py:21
  17.9 13.2 %collective-permute-start.11 = (bf16[4,32,1280]{2,1,0:T(8,128)(2,1)S(1)}, bf16[4,32,1280]{2,1,0:T(8,128)(2,1)S(1)}, u32[]{:S(2)}, u32[]{:S(2)}) collective-permute-start(bf16[4,32,1280]{2,1,0:T(8,128)(2,1)S(1)} %get-tuple-element.56), channel_id=1, source_target_pairs={{0,16},{1,17},{8,24},{9,25},{16,0},{17,1},{24,8},{25,9},{2,18},{3,... | collective-permute-start | bytes 983048 | tf_op jit(solution)/shard_map/ppermute | solution.py:31
  22.6 12.7 %all-to-all-start = ((f32[16,1,128]{2,1,0:T(1,128)}), f32[16,1,128]{2,1,0:T(1,128)S(1)}, u32[]{:S(2)}, u32[]{:S(2)}) async-start(f32[16,1,128]{2,1,0:T(1,128)} %broadcast_in_dim.126), calls=%async_computation | async-start | bytes 16384 | tf_op jit(solution)/shard_map/all_to_all | solution.py:287
  27.6 11.1 %collective-permute-start.7 = (bf16[4,32,1280]{2,1,0:T(8,128)(2,1)S(1)}, bf16[4,32,1280]{2,1,0:T(8,128)(2,1)}, u32[]{:S(2)}, u32[]{:S(2)}) collective-permute-start(bf16[4,32,1280]{2,1,0:T(8,128)(2,1)S(1)} %get-tuple-element.57), channel_id=1, source_target_pairs={{0,64},{1,65},{32,96},{33,97},{64,0},{65,1},{96,32},{97,33},{2,66}... | collective-permute-start | bytes 983048 | tf_op jit(solution)/shard_map/ppermute | solution.py:31
  31.1 7.6 %collective-permute-start.12 = (bf16[4,32,1280]{2,1,0:T(8,128)(2,1)S(1)}, bf16[4,32,1280]{2,1,0:T(8,128)(2,1)}, u32[]{:S(2)}, u32[]{:S(2)}) collective-permute-start(bf16[4,32,1280]{2,1,0:T(8,128)(2,1)S(1)} %collective-permute-done.11), channel_id=1, source_target_pairs={{0,1},{1,0},{2,3},{3,2},{4,5},{5,4},{6,7},{7,6},{8,9},{9,8},{10,11... | collective-permute-start | bytes 983048 | tf_op jit(solution)/shard_map/ppermute | solution.py:21
  31.2 11.9 %collective-permute-start.9 = (bf16[2,4,32,1280]{3,2,1,0:T(8,128)(2,1)S(1)}, bf16[2,4,32,1280]{3,2,1,0:T(8,128)(2,1)S(1)}, u32[]{:S(2)}, u32[]{:S(2)}) collective-permute-start(bf16[2,4,32,1280]{3,2,1,0:T(8,128)(2,1)S(1)} %get-tuple-element.30), channel_id=1, source_target_pairs={{0,8},{1,25},{8,16},{9,1},{16,24},{17,9},{24,0},{25,17},{2,10},{3,... | collective-permute-start | bytes 1966088 | tf_op jit(solution)/shard_map/ppermute | solution.py:26
  32.7 12.8 %collective-permute-start.5 = (bf16[2,4,32,1280]{3,2,1,0:T(8,128)(2,1)S(1)}, bf16[2,4,32,1280]{3,2,1,0:T(8,128)(2,1)S(1)}, u32[]{:S(2)}, u32[]{:S(2)}) collective-permute-start(bf16[2,4,32,1280]{3,2,1,0:T(8,128)(2,1)S(1)} %get-tuple-element.34), channel_id=1, source_target_pairs={{0,32},{1,97},{32,64},{33,1},{64,96},{65,33},{96,0},{97,65},{2,34}... | collective-permute-start | bytes 1966088 | tf_op jit(solution)/shard_map/ppermute | solution.py:26
  38.7 4.3 %collective-permute-start.8 = (bf16[4,32,1280]{2,1,0:T(8,128)(2,1)}, bf16[4,32,1280]{2,1,0:T(8,128)(2,1)S(1)}, u32[]{:S(2)}, u32[]{:S(2)}) collective-permute-start(bf16[4,32,1280]{2,1,0:T(8,128)(2,1)} %collective-permute-done.7), channel_id=1, source_target_pairs={{0,1},{1,0},{2,3},{3,2},{4,5},{5,4},{6,7},{7,6},{8,9},{9,8},{10,11... | collective-permute-start | bytes 983048 | tf_op jit(solution)/shard_map/ppermute | solution.py:21
  43.1 2.7 %collective-permute-start.10 = (bf16[2,4,32,1280]{3,2,1,0:T(8,128)(2,1)S(1)}, bf16[2,4,32,1280]{3,2,1,0:T(8,128)(2,1)S(1)}, u32[]{:S(2)}, u32[]{:S(2)}) collective-permute-start(bf16[2,4,32,1280]{3,2,1,0:T(8,128)(2,1)S(1)} %collective-permute-done.9), channel_id=1, source_target_pairs={{0,1},{1,0},{2,3},{3,2},{4,5},{5,4},{6,7},{7,6},{8,9},{9,8},{10,11... | collective-permute-start | bytes 1966088 | tf_op jit(solution)/shard_map/ppermute | solution.py:21
  45.6 2.1 %collective-permute-start.6 = (bf16[2,4,32,1280]{3,2,1,0:T(8,128)(2,1)S(1)}, bf16[2,4,32,1280]{3,2,1,0:T(8,128)(2,1)S(1)}, u32[]{:S(2)}, u32[]{:S(2)}) collective-permute-start(bf16[2,4,32,1280]{3,2,1,0:T(8,128)(2,1)S(1)} %collective-permute-done.5), channel_id=1, source_target_pairs={{0,1},{1,0},{2,3},{3,2},{4,5},{5,4},{6,7},{7,6},{8,9},{9,8},{10,11... | collective-permute-start | bytes 1966088 | tf_op jit(solution)/shard_map/ppermute | solution.py:21
  48.1 1.7 %copy-start.4 = (bf16[2,4,64,1280]{3,2,1,0:T(8,128)(2,1)}, bf16[2,4,64,1280]{3,2,1,0:T(8,128)(2,1)S(1)}, u32[]{:S(2)}) copy-start(bf16[2,4,64,1280]{3,2,1,0:T(8,128)(2,1)S(1)} %get-tuple-element.52.refs_1_) | copy-start | bytes 3932164
  48.1 21.7 %copy-start.3 = (bf16[2,4,64,1280]{3,2,1,0:T(8,128)(2,1)}, bf16[2,4,64,1280]{3,2,1,0:T(8,128)(2,1)S(1)}, u32[]{:S(2)}) copy-start(bf16[2,4,64,1280]{3,2,1,0:T(8,128)(2,1)S(1)} %get-tuple-element.53.refs_3_) | copy-start | bytes 3932164
  48.2 19.0 %collective-permute-start.17 = (bf16[2,4,64,1280]{3,2,1,0:T(8,128)(2,1)S(1)}, bf16[2,4,64,1280]{3,2,1,0:T(8,128)(2,1)}, u32[]{:S(2)}, u32[]{:S(2)}) collective-permute-start(bf16[2,4,64,1280]{3,2,1,0:T(8,128)(2,1)S(1)} %get-tuple-element.52.refs_1_), channel_id=1, source_target_pairs={{0,8},{1,25},{8,16},{9,1},{16,24},{17,9},{24,0},{25,17},{2,10},{3,... | collective-permute-start | bytes 3932168 | tf_op jit(solution)/shard_map/ppermute | solution.py:26
  50.1 17.0 %copy-start.6 = (bf16[2,4,64,1280]{3,2,1,0:T(8,128)(2,1)}, bf16[2,4,64,1280]{3,2,1,0:T(8,128)(2,1)S(1)}, u32[]{:S(2)}) copy-start(bf16[2,4,64,1280]{3,2,1,0:T(8,128)(2,1)S(1)} %get-tuple-element.54.refs_0_) | copy-start | bytes 3932164
  50.1 25.4 %copy-start.5 = (bf16[2,4,64,1280]{3,2,1,0:T(8,128)(2,1)}, bf16[2,4,64,1280]{3,2,1,0:T(8,128)(2,1)S(1)}, u32[]{:S(2)}) copy-start(bf16[2,4,64,1280]{3,2,1,0:T(8,128)(2,1)S(1)} %get-tuple-element.55.refs_2_) | copy-start | bytes 3932164
  50.2 19.0 %collective-permute-start.15 = (bf16[2,4,64,1280]{3,2,1,0:T(8,128)(2,1)S(1)}, bf16[2,4,64,1280]{3,2,1,0:T(8,128)(2,1)}, u32[]{:S(2)}, u32[]{:S(2)}) collective-permute-start(bf16[2,4,64,1280]{3,2,1,0:T(8,128)(2,1)S(1)} %get-tuple-element.54.refs_0_), channel_id=1, source_target_pairs={{0,32},{1,97},{32,64},{33,1},{64,96},{65,33},{96,0},{97,65},{2,34}... | collective-permute-start | bytes 3932168 | tf_op jit(solution)/shard_map/ppermute | solution.py:26
  67.2 5.6 %collective-permute-start.20 = (bf16[2,4,64,1280]{3,2,1,0:T(8,128)(2,1)}, bf16[2,4,64,1280]{3,2,1,0:T(8,128)(2,1)}, u32[]{:S(2)}, u32[]{:S(2)}) collective-permute-start(bf16[2,4,64,1280]{3,2,1,0:T(8,128)(2,1)} %collective-permute-done.17.refs_5_), channel_id=1, source_target_pairs={{0,1},{1,0},{2,3},{3,2},{4,5},{5,4},{6,7},{7,6},{8,9},{9,8},{10,11... | collective-permute-start | bytes 3932168 | tf_op jit(solution)/shard_map/ppermute | solution.py:21
  69.1 6.4 %collective-permute-start.19 = (bf16[2,4,64,1280]{3,2,1,0:T(8,128)(2,1)}, bf16[2,4,64,1280]{3,2,1,0:T(8,128)(2,1)}, u32[]{:S(2)}, u32[]{:S(2)}) collective-permute-start(bf16[2,4,64,1280]{3,2,1,0:T(8,128)(2,1)} %collective-permute-done.15.refs_4_), channel_id=1, source_target_pairs={{0,1},{1,0},{2,3},{3,2},{4,5},{5,4},{6,7},{7,6},{8,9},{9,8},{10,11... | collective-permute-start | bytes 3932168 | tf_op jit(solution)/shard_map/ppermute | solution.py:21
  69.8 29.1 %collective-permute-start.14 = (bf16[2,4,64,1280]{3,2,1,0:T(8,128)(2,1)S(1)}, bf16[2,4,64,1280]{3,2,1,0:T(8,128)(2,1)}, u32[]{:S(2)}, u32[]{:S(2)}) collective-permute-start(bf16[2,4,64,1280]{3,2,1,0:T(8,128)(2,1)S(1)} %get-tuple-element.53.refs_3_), channel_id=1, source_target_pairs={{0,8},{1,25},{8,16},{9,1},{16,24},{17,9},{24,0},{25,17},{2,10},{3,... | collective-permute-start | bytes 3932168 | tf_op jit(solution)/shard_map/ppermute | solution.py:26
  71.4 27.6 %collective-permute-start.13 = (bf16[2,4,64,1280]{3,2,1,0:T(8,128)(2,1)S(1)}, bf16[2,4,64,1280]{3,2,1,0:T(8,128)(2,1)}, u32[]{:S(2)}, u32[]{:S(2)}) collective-permute-start(bf16[2,4,64,1280]{3,2,1,0:T(8,128)(2,1)S(1)} %get-tuple-element.55.refs_2_), channel_id=1, source_target_pairs={{0,32},{1,97},{32,64},{33,1},{64,96},{65,33},{96,0},{97,65},{2,34}... | collective-permute-start | bytes 3932168 | tf_op jit(solution)/shard_map/ppermute | solution.py:26
  71.6 31.2 %collective-permute-start.18 = (bf16[2,4,64,1280]{3,2,1,0:T(8,128)(2,1)}, bf16[2,4,64,1280]{3,2,1,0:T(8,128)(2,1)}, u32[]{:S(2)}, u32[]{:S(2)}) collective-permute-start(bf16[2,4,64,1280]{3,2,1,0:T(8,128)(2,1)} %collective-permute-done.17.refs_5_), channel_id=1, source_target_pairs={{0,8},{1,25},{8,16},{9,1},{16,24},{17,9},{24,0},{25,17},{2,10},{3,... | collective-permute-start | bytes 3932168 | tf_op jit(solution)/shard_map/ppermute | solution.py:26
  72.8 31.5 %collective-permute-start.16 = (bf16[2,4,64,1280]{3,2,1,0:T(8,128)(2,1)}, bf16[2,4,64,1280]{3,2,1,0:T(8,128)(2,1)}, u32[]{:S(2)}, u32[]{:S(2)}) collective-permute-start(bf16[2,4,64,1280]{3,2,1,0:T(8,128)(2,1)} %collective-permute-done.15.refs_4_), channel_id=1, source_target_pairs={{0,32},{1,97},{32,64},{33,1},{64,96},{65,33},{96,0},{97,65},{2,34}... | collective-permute-start | bytes 3932168 | tf_op jit(solution)/shard_map/ppermute | solution.py:26
  75.5 30.2 %copy-start = (s32[16,64,1]{2,1,0:T(8,128)S(1)}, s32[16,64,1]{2,1,0:T(8,128)}, u32[]{:S(2)}) copy-start(s32[16,64,1]{2,1,0:T(8,128)} %copy.67.ids_ref) | copy-start | bytes 12292
  75.5 30.2 %copy-start.2 = (s32[4]{0:T(128)S(1)}, s32[4]{0:T(128)}, u32[]{:S(2)}) copy-start(s32[4]{0:T(128)} %pad_add_fusion.where_ref) | copy-start | bytes 52
  104.3 16.5 %collective-permute-start.21 = (bf16[2,4,64,1280]{3,2,1,0:T(8,128)(2,1)}, bf16[2,4,64,1280]{3,2,1,0:T(8,128)(2,1)}, u32[]{:S(2)}, u32[]{:S(2)}) collective-permute-start(bf16[2,4,64,1280]{3,2,1,0:T(8,128)(2,1)} %collective-permute-done.13.refs_0_), channel_id=1, source_target_pairs={{0,1},{1,0},{2,3},{3,2},{4,5},{5,4},{6,7},{7,6},{8,9},{9,8},{10,11... | collective-permute-start | bytes 3932168 | tf_op jit(solution)/shard_map/ppermute | solution.py:21
  104.3 16.5 %collective-permute-start.22 = (bf16[2,4,64,1280]{3,2,1,0:T(8,128)(2,1)}, bf16[2,4,64,1280]{3,2,1,0:T(8,128)(2,1)}, u32[]{:S(2)}, u32[]{:S(2)}) collective-permute-start(bf16[2,4,64,1280]{3,2,1,0:T(8,128)(2,1)} %collective-permute-done.14.refs_1_), channel_id=1, source_target_pairs={{0,1},{1,0},{2,3},{3,2},{4,5},{5,4},{6,7},{7,6},{8,9},{9,8},{10,11... | collective-permute-start | bytes 3932168 | tf_op jit(solution)/shard_map/ppermute | solution.py:21
  104.9 16.0 %collective-permute-start.23 = (bf16[2,4,64,1280]{3,2,1,0:T(8,128)(2,1)}, bf16[2,4,64,1280]{3,2,1,0:T(8,128)(2,1)}, u32[]{:S(2)}, u32[]{:S(2)}) collective-permute-start(bf16[2,4,64,1280]{3,2,1,0:T(8,128)(2,1)} %collective-permute-done.16.refs_2_), channel_id=1, source_target_pairs={{0,1},{1,0},{2,3},{3,2},{4,5},{5,4},{6,7},{7,6},{8,9},{9,8},{10,11... | collective-permute-start | bytes 3932168 | tf_op jit(solution)/shard_map/ppermute | solution.py:21
  104.9 16.0 %collective-permute-start.24 = (bf16[2,4,64,1280]{3,2,1,0:T(8,128)(2,1)}, bf16[2,4,64,1280]{3,2,1,0:T(8,128)(2,1)}, u32[]{:S(2)}, u32[]{:S(2)}) collective-permute-start(bf16[2,4,64,1280]{3,2,1,0:T(8,128)(2,1)} %collective-permute-done.18.refs_3_), channel_id=1, source_target_pairs={{0,1},{1,0},{2,3},{3,2},{4,5},{5,4},{6,7},{7,6},{8,9},{9,8},{10,11... | collective-permute-start | bytes 3932168 | tf_op jit(solution)/shard_map/ppermute | solution.py:21
  105.7 0.8 copy-start.1
  131.9 17.0 %copy-start.8 = (s32[2,32]{1,0:T(2,128)S(1)}, s32[2,32]{1,0:T(2,128)}, u32[]{:S(2)}) copy-start(s32[2,32]{1,0:T(2,128)} %param.15) | copy-start | bytes 772
  132.0 17.0 %copy-start.9 = (s32[2,32]{1,0:T(2,128)S(1)}, s32[2,32]{1,0:T(2,128)}, u32[]{:S(2)}) copy-start(s32[2,32]{1,0:T(2,128)} %param.14) | copy-start | bytes 772
  132.0 17.0 %copy-start.10 = (f32[2,32]{1,0:T(2,128)S(1)}, f32[2,32]{1,0:T(2,128)}, u32[]{:S(2)}) copy-start(f32[2,32]{1,0:T(2,128)} %param.16) | copy-start | bytes 772
  132.9 15.6 %all-to-all-start.1 = ((f32[128,1,256]{2,1,0:T(1,128)}), f32[128,1,256]{2,1,0:T(1,128)S(1)}, u32[]{:S(2)}, u32[]{:S(2)}) async-start(f32[128,1,256]{2,1,0:T(1,128)} %copy.68), calls=%async_computation.1 | async-start | bytes 262144 | tf_op jit(solution)/shard_map/all_to_all | solution.py:335
  150.4 11.0 %all-to-all-start.2 = ((f32[16,1,2]{2,1,0:T(1,128)}), f32[16,1,2]{2,1,0:T(1,128)S(1)}, u32[]{:S(2)}, u32[]{:S(2)}) async-start(f32[16,1,2]{2,1,0:T(1,128)} %broadcast_in_dim.139), calls=%async_computation.2 | async-start | bytes 16384 | tf_op jit(solution)/shard_map/all_to_all | solution.py:349

commit v4 on v3

--- a/solution.py
+++ b/solution.py
@@ -50,7 +50,7 @@
 
 
 def row_stats(logits, ids, packed):
-    chunk = 64
+    chunk = 256
     lane = lax.broadcasted_iota(jnp.int32, (chunk, 128), 1)
     tiles = range(0, logits.shape[2], 128)
 
@@ -115,7 +115,7 @@
 
 
 class HeadBlocks:
-    ahead = 4
+    ahead = 6
 
     def __init__(self, heads, near_to, buffer, sems):
         self.order = [(m, j) for m in range(2) for j in range(4)]
@@ -271,6 +271,7 @@
 
     both = jnp.stack([hidden_policy.reshape(64, 640), hidden_ref.reshape(64, 640)])
     got = swap_cores(both)
+    got, done_flags = lax.optimization_barrier((got, done_flags))
     rest = jnp.concatenate([jnp.where(first, both, got), jnp.where(first, got, both)], axis=-1)
 
     mask = response_mask.astype(jnp.float32)

time: 163 us -> 161 us (0.988)
  Pallas kernels: 48.7 us -> 45.6 us
    pallas_call x3, Pallas kernels: 48.7 us -> 45.6 us  [stats_call(): pl.pallas_call(functools.partial(kernel, tuple((p for _, p in pieces))),...]
  transfers between devices with their start and end apart: 28 -> 28, of which waited for: 14 -> 15; matrix products, arithmetic and copies ran while one was open for 6% -> 6% of each run, Pallas kernels for 23% -> 22%
where the time goes in v4:
time: 161 us; the launch traced here: 160 us
  waiting for transfers between devices  59.4 us (37%)
  Pallas kernels  45.6 us (28%)
  starting transfers between devices  37.1 us (23%)
  other arithmetic  10.4 us (6%)
  local copies, waits for them, and re-layouts  6.55 us (4%)
    pallas_call x3, Pallas kernels, stats_call(): pl.pallas_call(functools.partial(kernel, tuple((p for _, p in pieces))),...  45.6 us
    ppermute x9, waiting for transfers between devices, near(): return lax.ppermute(value, (axis, 'core'), pairs)  32.3 us
    ppermute x3, starting transfers between devices, far(): return lax.ppermute(value, (axis, 'core'), pairs)  10.6 us
    ppermute x9, starting transfers between devices, near(): return lax.ppermute(value, (axis, 'core'), pairs)  10.2 us
    all_to_all x1, waiting for transfers between devices, body(): stats = lax.all_to_all(stats, ALL, 0, 0, tiled=True).reshape(128, 4, 2, tok)  9.09 us
    all_to_all x1, waiting for transfers between devices, body(): lax.all_to_all(jnp.broadcast_to(local_gae[:, 0][None], (16, 2)), PLANE, 0...  6.96 us
    all_to_all x1, starting transfers between devices, body(): stats = lax.all_to_all(stats, ALL, 0, 0, tiled=True).reshape(128, 4, 2, tok)  6.54 us
    ppermute x3, waiting for transfers between devices, far(): return lax.ppermute(value, (axis, 'core'), pairs)  5.29 us
  transfers between devices with their start and end apart: 28, of which 15 were waited for; matrix products, arithmetic and copies ran while one was open for 6% of the time, Pallas kernels for 22%

profile of v4, /device:TPU:0, one launch (start us, length us, event | category | flops | bytes accessed | tf_op | source)
XLA Modules:
  0.0 160.3 jit_solution(17668811537114323492)
XLA Ops:
  0.6 1.0 pad_maximum_fusion.4
  1.7 0.7 convert_element_type.22
  2.5 0.6 collective-permute-done
  3.1 1.0 broadcast_select_fusion.8
  4.2 3.2 %collective-permute-start.3 = (bf16[64,1280]{1,0:T(8,128)(2,1)S(1)}, bf16[64,1280]{1,0:T(8,128)(2,1)S(1)}, u32[]{:S(2)}, u32[]{:S(2)}) collective-permute-start(bf16[64,1280]{1,0:T(8,128)(2,1)S(1)} %fusion.2), channel_id=1, source_target_pairs={{0,4},{1,5},{2,6},{3,7},{4,0},{5,1},{6,2},{7,3},{8,12},{9,13},{10,... | collective-permute-start | bytes 491528 | tf_op jit(solution)/shard_map/ppermute | solution.py:31
  7.3 0.6 collective-permute-start.1
  8.8 3.2 %collective-permute-done.3 = bf16[64,1280]{1,0:T(8,128)(2,1)S(1)} collective-permute-done((bf16[64,1280]{1,0:T(8,128)(2,1)S(1)}, bf16[64,1280]{1,0:T(8,128)(2,1)S(1)}, u32[]{:S(2)}, u32[]{:S(2)}) %collective-permute-start.3) | collective-permute-done | bytes 163872 | tf_op jit(solution)/shard_map/ppermute | solution.py:31
  12.1 3.6 %collective-permute-done.1 = bf16[2,64,1280]{2,1,0:T(8,128)(2,1)S(1)} collective-permute-done((bf16[2,64,1280]{2,1,0:T(8,128)(2,1)S(1)}, bf16[2,64,1280]{2,1,0:T(8,128)(2,1)S(1)}, u32[]{:S(2)}, u32[]{:S(2)}) %collective-permute-start.1) | collective-permute-done | bytes 327712 | tf_op jit(solution)/shard_map/ppermute | solution.py:26
  15.8 1.4 collective-permute-done.2
  17.6 4.0 %collective-permute-start.11 = (bf16[4,32,1280]{2,1,0:T(8,128)(2,1)S(1)}, bf16[4,32,1280]{2,1,0:T(8,128)(2,1)S(1)}, u32[]{:S(2)}, u32[]{:S(2)}) collective-permute-start(bf16[4,32,1280]{2,1,0:T(8,128)(2,1)S(1)} %get-tuple-element.60), channel_id=1, source_target_pairs={{0,16},{1,17},{8,24},{9,25},{16,0},{17,1},{24,8},{25,9},{2,18},{3,... | collective-permute-start | bytes 983048 | tf_op jit(solution)/shard_map/ppermute | solution.py:31
  21.6 0.6 broadcast_in_dim.126
  22.2 5.0 %all-to-all-start = ((f32[16,1,128]{2,1,0:T(1,128)}), f32[16,1,128]{2,1,0:T(1,128)S(1)}, u32[]{:S(2)}, u32[]{:S(2)}) async-start(f32[16,1,128]{2,1,0:T(1,128)} %broadcast_in_dim.126), calls=%async_computation | async-start | bytes 16384 | tf_op jit(solution)/shard_map/all_to_all | solution.py:288
  27.2 3.4 %collective-permute-start.7 = (bf16[4,32,1280]{2,1,0:T(8,128)(2,1)S(1)}, bf16[4,32,1280]{2,1,0:T(8,128)(2,1)}, u32[]{:S(2)}, u32[]{:S(2)}) collective-permute-start(bf16[4,32,1280]{2,1,0:T(8,128)(2,1)S(1)} %get-tuple-element.61), channel_id=1, source_target_pairs={{0,64},{1,65},{32,96},{33,97},{64,0},{65,1},{96,32},{97,33},{2,66}... | collective-permute-start | bytes 983048 | tf_op jit(solution)/shard_map/ppermute | solution.py:31
  30.8 1.5 collective-permute-start.9
  32.3 0.6 collective-permute-start.5
  32.9 2.0 %all-to-all-done = f32[16,1,128]{2,1,0:T(1,128)S(1)} async-done(((f32[16,1,128]{2,1,0:T(1,128)}), f32[16,1,128]{2,1,0:T(1,128)S(1)}, u32[]{:S(2)}, u32[]{:S(2)}) %all-to-all-start) | async-done | bytes 8224 | tf_op jit(solution)/shard_map/all_to_all | solution.py:288
  34.9 0.5 broadcast.76
  35.4 0.7 reduce.11
  36.2 2.1 %collective-permute-done.7 = bf16[4,32,1280]{2,1,0:T(8,128)(2,1)} collective-permute-done((bf16[4,32,1280]{2,1,0:T(8,128)(2,1)S(1)}, bf16[4,32,1280]{2,1,0:T(8,128)(2,1)}, u32[]{:S(2)}, u32[]{:S(2)}) %collective-permute-start.7) | collective-permute-done | bytes 327712 | tf_op jit(solution)/shard_map/ppermute | solution.py:31
  38.3 1.0 select_bitcast_fusion.1
  39.4 3.2 %collective-permute-done.9 = bf16[2,4,32,1280]{3,2,1,0:T(8,128)(2,1)S(1)} collective-permute-done((bf16[2,4,32,1280]{3,2,1,0:T(8,128)(2,1)S(1)}, bf16[2,4,32,1280]{3,2,1,0:T(8,128)(2,1)S(1)}, u32[]{:S(2)}, u32[]{:S(2)}) %collective-permute-start.9) | collective-permute-done | bytes 655392 | tf_op jit(solution)/shard_map/ppermute | solution.py:26
  42.6 1.0 select_bitcast_fusion.4
  43.7 1.5 collective-permute-done.5
  45.5 1.7 %collective-permute-done.6 = bf16[2,4,32,1280]{3,2,1,0:T(8,128)(2,1)S(1)} collective-permute-done((bf16[2,4,32,1280]{3,2,1,0:T(8,128)(2,1)S(1)}, bf16[2,4,32,1280]{3,2,1,0:T(8,128)(2,1)S(1)}, u32[]{:S(2)}, u32[]{:S(2)}) %collective-permute-start.6) | collective-permute-done | bytes 655392 | tf_op jit(solution)/shard_map/ppermute | solution.py:21
  47.7 1.6 collective-permute-start.17
  49.7 1.5 collective-permute-start.15
  51.3 15.5 %collective-permute-done.17.refs_5_ = bf16[2,4,64,1280]{3,2,1,0:T(8,128)(2,1)} collective-permute-done((bf16[2,4,64,1280]{3,2,1,0:T(8,128)(2,1)S(1)}, bf16[2,4,64,1280]{3,2,1,0:T(8,128)(2,1)}, u32[]{:S(2)}, u32[]{:S(2)}) %collective-permute-start.17) | collective-permute-done | bytes 1310752 | tf_op jit(solution)/shard_map/ppermute | solution.py:26
  66.7 2.0 %collective-permute-done.15.refs_4_ = bf16[2,4,64,1280]{3,2,1,0:T(8,128)(2,1)} collective-permute-done((bf16[2,4,64,1280]{3,2,1,0:T(8,128)(2,1)S(1)}, bf16[2,4,64,1280]{3,2,1,0:T(8,128)(2,1)}, u32[]{:S(2)}, u32[]{:S(2)}) %collective-permute-start.15) | collective-permute-done | bytes 1310752 | tf_op jit(solution)/shard_map/ppermute | solution.py:26
  68.8 0.6 pad_add_fusion.where_ref
  69.4 1.5 collective-permute-start.14
  71.2 1.2 collective-permute-start.18
  72.4 1.4 collective-permute-start.16
  74.1 1.1 copy.67.ids_ref
  75.1 22.2 %early_stats.1.refs_6_ = f32[16,8,128]{2,1,0:T(8,128)} custom-call(s32[4]{0:T(128)} %pad_add_fusion.where_ref, s32[16,64,1]{2,1,0:T(8,128)} %copy.67.ids_ref, bf16[2,4,64,1280]{3,2,1,0:T(8,128)(2,1)} %copy-done.6, bf16[2,4,64,1280]{3,2,1,0:T(8,128)(2,1)} %copy-done.4, bf16[2,4,64,1280]{3,2,1,0:T(8,128)(2,1)} %copy-done.5, ...), custom_call_target="tpu_custom_call" | custom-call | flops 12079595520 | bytes 34078720 | tf_op jit(solution)/shard_map/early_stats/pallas_call | solution.py:220
  97.3 5.1 %collective-permute-done.18.refs_3_ = bf16[2,4,64,1280]{3,2,1,0:T(8,128)(2,1)} collective-permute-done((bf16[2,4,64,1280]{3,2,1,0:T(8,128)(2,1)}, bf16[2,4,64,1280]{3,2,1,0:T(8,128)(2,1)}, u32[]{:S(2)}, u32[]{:S(2)}) %collective-permute-start.18) | collective-permute-done | bytes 1310752 | tf_op jit(solution)/shard_map/ppermute | solution.py:26
  102.5 1.5 collective-permute-done.16.refs_2_
  105.3 0.8 copy-done.1
  106.1 13.4 %late_stats.1 = (f32[16,8,128]{2,1,0:T(8,128)S(1)}, bf16[5120,1152]{1,0:T(8,128)(2,1)S(1)}, bf16[5120,1152]{1,0:T(8,128)(2,1)S(1)}) custom-call(s32[4]{0:T(128)S(1)} %copy-done.2, s32[16,64,1]{2,1,0:T(8,128)S(1)} %copy-done, bf16[2,4,64,1280]{3,2,1,0:T(8,128)(2,1)} %collective-permute-done.13.refs_0_, ...), custom_call_target="tpu_custom_call", output_to_operand_aliasing={{0}: (8, {})} | custom-call | flops 6039797760 | bytes 28835840 | tf_op jit(solution)/shard_map/late_stats/pallas_call | solution.py:220
  119.5 10.1 %last_stats.1 = f32[16,8,128]{2,1,0:T(8,128)S(1)} custom-call(s32[4]{0:T(128)S(1)} %copy-done.2, s32[16,64,1]{2,1,0:T(8,128)S(1)} %copy-done, bf16[2,4,64,1280]{3,2,1,0:T(8,128)(2,1)} %collective-permute-done.21.refs_0_, bf16[2,4,64,1280]{3,2,1,0:T(8,128)(2,1)} %collective-permute-done.22.refs_1_, ...), custom_call_target="tpu_custom_call", output_to_operand_aliasing={{}: (8, {})} | custom-call | flops 6039797760 | bytes 28835840 | tf_op jit(solution)/shard_map/last_stats/pallas_call | solution.py:220
  129.7 0.8 copy.68
  130.5 6.5 %all-to-all-start.1 = ((f32[128,1,256]{2,1,0:T(1,128)}), f32[128,1,256]{2,1,0:T(1,128)S(1)}, u32[]{:S(2)}, u32[]{:S(2)}) async-start(f32[128,1,256]{2,1,0:T(1,128)} %copy.68), calls=%async_computation.1 | async-start | bytes 262144 | tf_op jit(solution)/shard_map/all_to_all | solution.py:336
  137.4 9.1 %all-to-all-done.1 = f32[128,1,256]{2,1,0:T(1,128)S(1)} async-done(((f32[128,1,256]{2,1,0:T(1,128)}), f32[128,1,256]{2,1,0:T(1,128)S(1)}, u32[]{:S(2)}, u32[]{:S(2)}) %all-to-all-start.1) | async-done | bytes 131104 | tf_op jit(solution)/shard_map/all_to_all | solution.py:336
  146.9 0.6 fusion.14
  147.8 0.6 broadcast_in_dim.139
  148.4 3.5 %all-to-all-start.2 = ((f32[16,1,2]{2,1,0:T(1,128)}), f32[16,1,2]{2,1,0:T(1,128)S(1)}, u32[]{:S(2)}, u32[]{:S(2)}) async-start(f32[16,1,2]{2,1,0:T(1,128)} %broadcast_in_dim.139), calls=%async_computation.2 | async-start | bytes 16384 | tf_op jit(solution)/shard_map/all_to_all | solution.py:350
  151.9 0.6 fusion.18
  152.5 7.0 %all-to-all-done.2 = f32[16,1,2]{2,1,0:T(1,128)S(1)} async-done(((f32[16,1,2]{2,1,0:T(1,128)}), f32[16,1,2]{2,1,0:T(1,128)S(1)}, u32[]{:S(2)}, u32[]{:S(2)}) %all-to-all-start.2) | async-done | bytes 160 | tf_op jit(solution)/shard_map/all_to_all | solution.py:350
  159.6 0.6 add_multiply_fusion
  (119 shorter events, 6.5 us)
Async XLA Ops:
  0.6 7.3 %copy-start.8 = (s32[2,32]{1,0:T(2,128)S(1)}, s32[2,32]{1,0:T(2,128)}, u32[]{:S(2)}) copy-start(s32[2,32]{1,0:T(2,128)} %param.15) | copy-start | bytes 772
  1.6 1.5 collective-permute-start
  4.0 8.0 %copy-start.7 = (f32[2,32]{1,0:T(2,128)S(1)}, f32[2,32]{1,0:T(2,128)}, u32[]{:S(2)}) copy-start(f32[2,32]{1,0:T(2,128)} %param.17) | copy-start | bytes 772
  4.2 7.8 %collective-permute-start.3 = (bf16[64,1280]{1,0:T(8,128)(2,1)S(1)}, bf16[64,1280]{1,0:T(8,128)(2,1)S(1)}, u32[]{:S(2)}, u32[]{:S(2)}) collective-permute-start(bf16[64,1280]{1,0:T(8,128)(2,1)S(1)} %fusion.2), channel_id=1, source_target_pairs={{0,4},{1,5},{2,6},{3,7},{4,0},{5,1},{6,2},{7,3},{8,12},{9,13},{10,... | collective-permute-start | bytes 491528 | tf_op jit(solution)/shard_map/ppermute | solution.py:31
  7.3 8.3 %collective-permute-start.1 = (bf16[2,64,1280]{2,1,0:T(8,128)(2,1)S(1)}, bf16[2,64,1280]{2,1,0:T(8,128)(2,1)S(1)}, u32[]{:S(2)}, u32[]{:S(2)}) collective-permute-start(bf16[2,64,1280]{2,1,0:T(8,128)(2,1)S(1)} %get-tuple-element.75), channel_id=1, source_target_pairs={{0,2},{1,7},{2,4},{3,1},{4,6},{5,3},{6,0},{7,5},{8,10},{9,15},{10,... | collective-permute-start | bytes 983048 | tf_op jit(solution)/shard_map/ppermute | solution.py:26
  12.0 3.8 %collective-permute-start.4 = (bf16[64,1280]{1,0:T(8,128)(2,1)S(1)}, bf16[64,1280]{1,0:T(8,128)(2,1)S(1)}, u32[]{:S(2)}, u32[]{:S(2)}) collective-permute-start(bf16[64,1280]{1,0:T(8,128)(2,1)S(1)} %collective-permute-done.3), channel_id=1, source_target_pairs={{0,1},{1,0},{2,3},{3,2},{4,5},{5,4},{6,7},{7,6},{8,9},{9,8},{10,11... | collective-permute-start | bytes 491528 | tf_op jit(solution)/shard_map/ppermute | solution.py:21
  15.6 1.6 %collective-permute-start.2 = (bf16[2,64,1280]{2,1,0:T(8,128)(2,1)S(1)}, bf16[2,64,1280]{2,1,0:T(8,128)(2,1)S(1)}, u32[]{:S(2)}, u32[]{:S(2)}) collective-permute-start(bf16[2,64,1280]{2,1,0:T(8,128)(2,1)S(1)} %collective-permute-done.1), channel_id=1, source_target_pairs={{0,1},{1,0},{2,3},{3,2},{4,5},{5,4},{6,7},{7,6},{8,9},{9,8},{10,11... | collective-permute-start | bytes 983048 | tf_op jit(solution)/shard_map/ppermute | solution.py:21
  17.6 13.1 %collective-permute-start.11 = (bf16[4,32,1280]{2,1,0:T(8,128)(2,1)S(1)}, bf16[4,32,1280]{2,1,0:T(8,128)(2,1)S(1)}, u32[]{:S(2)}, u32[]{:S(2)}) collective-permute-start(bf16[4,32,1280]{2,1,0:T(8,128)(2,1)S(1)} %get-tuple-element.60), channel_id=1, source_target_pairs={{0,16},{1,17},{8,24},{9,25},{16,0},{17,1},{24,8},{25,9},{2,18},{3,... | collective-permute-start | bytes 983048 | tf_op jit(solution)/shard_map/ppermute | solution.py:31
  22.2 12.7 %all-to-all-start = ((f32[16,1,128]{2,1,0:T(1,128)}), f32[16,1,128]{2,1,0:T(1,128)S(1)}, u32[]{:S(2)}, u32[]{:S(2)}) async-start(f32[16,1,128]{2,1,0:T(1,128)} %broadcast_in_dim.126), calls=%async_computation | async-start | bytes 16384 | tf_op jit(solution)/shard_map/all_to_all | solution.py:288
  27.2 11.1 %collective-permute-start.7 = (bf16[4,32,1280]{2,1,0:T(8,128)(2,1)S(1)}, bf16[4,32,1280]{2,1,0:T(8,128)(2,1)}, u32[]{:S(2)}, u32[]{:S(2)}) collective-permute-start(bf16[4,32,1280]{2,1,0:T(8,128)(2,1)S(1)} %get-tuple-element.61), channel_id=1, source_target_pairs={{0,64},{1,65},{32,96},{33,97},{64,0},{65,1},{96,32},{97,33},{2,66}... | collective-permute-start | bytes 983048 | tf_op jit(solution)/shard_map/ppermute | solution.py:31
  30.7 7.6 %collective-permute-start.12 = (bf16[4,32,1280]{2,1,0:T(8,128)(2,1)S(1)}, bf16[4,32,1280]{2,1,0:T(8,128)(2,1)}, u32[]{:S(2)}, u32[]{:S(2)}) collective-permute-start(bf16[4,32,1280]{2,1,0:T(8,128)(2,1)S(1)} %collective-permute-done.11), channel_id=1, source_target_pairs={{0,1},{1,0},{2,3},{3,2},{4,5},{5,4},{6,7},{7,6},{8,9},{9,8},{10,11... | collective-permute-start | bytes 983048 | tf_op jit(solution)/shard_map/ppermute | solution.py:21
  30.8 11.9 %collective-permute-start.9 = (bf16[2,4,32,1280]{3,2,1,0:T(8,128)(2,1)S(1)}, bf16[2,4,32,1280]{3,2,1,0:T(8,128)(2,1)S(1)}, u32[]{:S(2)}, u32[]{:S(2)}) collective-permute-start(bf16[2,4,32,1280]{3,2,1,0:T(8,128)(2,1)S(1)} %get-tuple-element.34), channel_id=1, source_target_pairs={{0,8},{1,25},{8,16},{9,1},{16,24},{17,9},{24,0},{25,17},{2,10},{3,... | collective-permute-start | bytes 1966088 | tf_op jit(solution)/shard_map/ppermute | solution.py:26
  32.3 12.8 %collective-permute-start.5 = (bf16[2,4,32,1280]{3,2,1,0:T(8,128)(2,1)S(1)}, bf16[2,4,32,1280]{3,2,1,0:T(8,128)(2,1)S(1)}, u32[]{:S(2)}, u32[]{:S(2)}) collective-permute-start(bf16[2,4,32,1280]{3,2,1,0:T(8,128)(2,1)S(1)} %get-tuple-element.38), channel_id=1, source_target_pairs={{0,32},{1,97},{32,64},{33,1},{64,96},{65,33},{96,0},{97,65},{2,34}... | collective-permute-start | bytes 1966088 | tf_op jit(solution)/shard_map/ppermute | solution.py:26
  38.3 4.3 %collective-permute-start.8 = (bf16[4,32,1280]{2,1,0:T(8,128)(2,1)}, bf16[4,32,1280]{2,1,0:T(8,128)(2,1)S(1)}, u32[]{:S(2)}, u32[]{:S(2)}) collective-permute-start(bf16[4,32,1280]{2,1,0:T(8,128)(2,1)} %collective-permute-done.7), channel_id=1, source_target_pairs={{0,1},{1,0},{2,3},{3,2},{4,5},{5,4},{6,7},{7,6},{8,9},{9,8},{10,11... | collective-permute-start | bytes 983048 | tf_op jit(solution)/shard_map/ppermute | solution.py:21
  42.6 2.7 %collective-permute-start.10 = (bf16[2,4,32,1280]{3,2,1,0:T(8,128)(2,1)S(1)}, bf16[2,4,32,1280]{3,2,1,0:T(8,128)(2,1)S(1)}, u32[]{:S(2)}, u32[]{:S(2)}) collective-permute-start(bf16[2,4,32,1280]{3,2,1,0:T(8,128)(2,1)S(1)} %collective-permute-done.9), channel_id=1, source_target_pairs={{0,1},{1,0},{2,3},{3,2},{4,5},{5,4},{6,7},{7,6},{8,9},{9,8},{10,11... | collective-permute-start | bytes 1966088 | tf_op jit(solution)/shard_map/ppermute | solution.py:21
  45.1 2.1 %collective-permute-start.6 = (bf16[2,4,32,1280]{3,2,1,0:T(8,128)(2,1)S(1)}, bf16[2,4,32,1280]{3,2,1,0:T(8,128)(2,1)S(1)}, u32[]{:S(2)}, u32[]{:S(2)}) collective-permute-start(bf16[2,4,32,1280]{3,2,1,0:T(8,128)(2,1)S(1)} %collective-permute-done.5), channel_id=1, source_target_pairs={{0,1},{1,0},{2,3},{3,2},{4,5},{5,4},{6,7},{7,6},{8,9},{9,8},{10,11... | collective-permute-start | bytes 1966088 | tf_op jit(solution)/shard_map/ppermute | solution.py:21
  47.7 1.7 %copy-start.4 = (bf16[2,4,64,1280]{3,2,1,0:T(8,128)(2,1)}, bf16[2,4,64,1280]{3,2,1,0:T(8,128)(2,1)S(1)}, u32[]{:S(2)}) copy-start(bf16[2,4,64,1280]{3,2,1,0:T(8,128)(2,1)S(1)} %get-tuple-element.56.refs_1_) | copy-start | bytes 3932164
  47.7 21.7 %copy-start.3 = (bf16[2,4,64,1280]{3,2,1,0:T(8,128)(2,1)}, bf16[2,4,64,1280]{3,2,1,0:T(8,128)(2,1)S(1)}, u32[]{:S(2)}) copy-start(bf16[2,4,64,1280]{3,2,1,0:T(8,128)(2,1)S(1)} %get-tuple-element.57.refs_3_) | copy-start | bytes 3932164
  47.7 19.0 %collective-permute-start.17 = (bf16[2,4,64,1280]{3,2,1,0:T(8,128)(2,1)S(1)}, bf16[2,4,64,1280]{3,2,1,0:T(8,128)(2,1)}, u32[]{:S(2)}, u32[]{:S(2)}) collective-permute-start(bf16[2,4,64,1280]{3,2,1,0:T(8,128)(2,1)S(1)} %get-tuple-element.56.refs_1_), channel_id=1, source_target_pairs={{0,8},{1,25},{8,16},{9,1},{16,24},{17,9},{24,0},{25,17},{2,10},{3,... | collective-permute-start | bytes 3932168 | tf_op jit(solution)/shard_map/ppermute | solution.py:26
  49.7 17.0 %copy-start.6 = (bf16[2,4,64,1280]{3,2,1,0:T(8,128)(2,1)}, bf16[2,4,64,1280]{3,2,1,0:T(8,128)(2,1)S(1)}, u32[]{:S(2)}) copy-start(bf16[2,4,64,1280]{3,2,1,0:T(8,128)(2,1)S(1)} %get-tuple-element.58.refs_0_) | copy-start | bytes 3932164
  49.7 25.4 %copy-start.5 = (bf16[2,4,64,1280]{3,2,1,0:T(8,128)(2,1)}, bf16[2,4,64,1280]{3,2,1,0:T(8,128)(2,1)S(1)}, u32[]{:S(2)}) copy-start(bf16[2,4,64,1280]{3,2,1,0:T(8,128)(2,1)S(1)} %get-tuple-element.59.refs_2_) | copy-start | bytes 3932164
  49.7 19.0 %collective-permute-start.15 = (bf16[2,4,64,1280]{3,2,1,0:T(8,128)(2,1)S(1)}, bf16[2,4,64,1280]{3,2,1,0:T(8,128)(2,1)}, u32[]{:S(2)}, u32[]{:S(2)}) collective-permute-start(bf16[2,4,64,1280]{3,2,1,0:T(8,128)(2,1)S(1)} %get-tuple-element.58.refs_0_), channel_id=1, source_target_pairs={{0,32},{1,97},{32,64},{33,1},{64,96},{65,33},{96,0},{97,65},{2,34}... | collective-permute-start | bytes 3932168 | tf_op jit(solution)/shard_map/ppermute | solution.py:26
  66.7 5.6 %collective-permute-start.20 = (bf16[2,4,64,1280]{3,2,1,0:T(8,128)(2,1)}, bf16[2,4,64,1280]{3,2,1,0:T(8,128)(2,1)}, u32[]{:S(2)}, u32[]{:S(2)}) collective-permute-start(bf16[2,4,64,1280]{3,2,1,0:T(8,128)(2,1)} %collective-permute-done.17.refs_5_), channel_id=1, source_target_pairs={{0,1},{1,0},{2,3},{3,2},{4,5},{5,4},{6,7},{7,6},{8,9},{9,8},{10,11... | collective-permute-start | bytes 3932168 | tf_op jit(solution)/shard_map/ppermute | solution.py:21
  68.7 6.4 %collective-permute-start.19 = (bf16[2,4,64,1280]{3,2,1,0:T(8,128)(2,1)}, bf16[2,4,64,1280]{3,2,1,0:T(8,128)(2,1)}, u32[]{:S(2)}, u32[]{:S(2)}) collective-permute-start(bf16[2,4,64,1280]{3,2,1,0:T(8,128)(2,1)} %collective-permute-done.15.refs_4_), channel_id=1, source_target_pairs={{0,1},{1,0},{2,3},{3,2},{4,5},{5,4},{6,7},{7,6},{8,9},{9,8},{10,11... | collective-permute-start | bytes 3932168 | tf_op jit(solution)/shard_map/ppermute | solution.py:21
  69.4 27.9 %collective-permute-start.14 = (bf16[2,4,64,1280]{3,2,1,0:T(8,128)(2,1)S(1)}, bf16[2,4,64,1280]{3,2,1,0:T(8,128)(2,1)}, u32[]{:S(2)}, u32[]{:S(2)}) collective-permute-start(bf16[2,4,64,1280]{3,2,1,0:T(8,128)(2,1)S(1)} %get-tuple-element.57.refs_3_), channel_id=1, source_target_pairs={{0,8},{1,25},{8,16},{9,1},{16,24},{17,9},{24,0},{25,17},{2,10},{3,... | collective-permute-start | bytes 3932168 | tf_op jit(solution)/shard_map/ppermute | solution.py:26
  71.0 26.4 %collective-permute-start.13 = (bf16[2,4,64,1280]{3,2,1,0:T(8,128)(2,1)S(1)}, bf16[2,4,64,1280]{3,2,1,0:T(8,128)(2,1)}, u32[]{:S(2)}, u32[]{:S(2)}) collective-permute-start(bf16[2,4,64,1280]{3,2,1,0:T(8,128)(2,1)S(1)} %get-tuple-element.59.refs_2_), channel_id=1, source_target_pairs={{0,32},{1,97},{32,64},{33,1},{64,96},{65,33},{96,0},{97,65},{2,34}... | collective-permute-start | bytes 3932168 | tf_op jit(solution)/shard_map/ppermute | solution.py:26
  71.2 31.2 %collective-permute-start.18 = (bf16[2,4,64,1280]{3,2,1,0:T(8,128)(2,1)}, bf16[2,4,64,1280]{3,2,1,0:T(8,128)(2,1)}, u32[]{:S(2)}, u32[]{:S(2)}) collective-permute-start(bf16[2,4,64,1280]{3,2,1,0:T(8,128)(2,1)} %collective-permute-done.17.refs_5_), channel_id=1, source_target_pairs={{0,8},{1,25},{8,16},{9,1},{16,24},{17,9},{24,0},{25,17},{2,10},{3,... | collective-permute-start | bytes 3932168 | tf_op jit(solution)/shard_map/ppermute | solution.py:26
  72.4 31.5 %collective-permute-start.16 = (bf16[2,4,64,1280]{3,2,1,0:T(8,128)(2,1)}, bf16[2,4,64,1280]{3,2,1,0:T(8,128)(2,1)}, u32[]{:S(2)}, u32[]{:S(2)}) collective-permute-start(bf16[2,4,64,1280]{3,2,1,0:T(8,128)(2,1)} %collective-permute-done.15.refs_4_), channel_id=1, source_target_pairs={{0,32},{1,97},{32,64},{33,1},{64,96},{65,33},{96,0},{97,65},{2,34}... | collective-permute-start | bytes 3932168 | tf_op jit(solution)/shard_map/ppermute | solution.py:26
  75.1 30.2 %copy-start = (s32[16,64,1]{2,1,0:T(8,128)S(1)}, s32[16,64,1]{2,1,0:T(8,128)}, u32[]{:S(2)}) copy-start(s32[16,64,1]{2,1,0:T(8,128)} %copy.67.ids_ref) | copy-start | bytes 12292
  75.1 30.2 %copy-start.2 = (s32[4]{0:T(128)S(1)}, s32[4]{0:T(128)}, u32[]{:S(2)}) copy-start(s32[4]{0:T(128)} %pad_add_fusion.where_ref) | copy-start | bytes 52
  103.9 15.6 %collective-permute-start.21 = (bf16[2,4,64,1280]{3,2,1,0:T(8,128)(2,1)}, bf16[2,4,64,1280]{3,2,1,0:T(8,128)(2,1)}, u32[]{:S(2)}, u32[]{:S(2)}) collective-permute-start(bf16[2,4,64,1280]{3,2,1,0:T(8,128)(2,1)} %collective-permute-done.13.refs_0_), channel_id=1, source_target_pairs={{0,1},{1,0},{2,3},{3,2},{4,5},{5,4},{6,7},{7,6},{8,9},{9,8},{10,11... | collective-permute-start | bytes 3932168 | tf_op jit(solution)/shard_map/ppermute | solution.py:21
  103.9 15.6 %collective-permute-start.22 = (bf16[2,4,64,1280]{3,2,1,0:T(8,128)(2,1)}, bf16[2,4,64,1280]{3,2,1,0:T(8,128)(2,1)}, u32[]{:S(2)}, u32[]{:S(2)}) collective-permute-start(bf16[2,4,64,1280]{3,2,1,0:T(8,128)(2,1)} %collective-permute-done.14.refs_1_), channel_id=1, source_target_pairs={{0,1},{1,0},{2,3},{3,2},{4,5},{5,4},{6,7},{7,6},{8,9},{9,8},{10,11... | collective-permute-start | bytes 3932168 | tf_op jit(solution)/shard_map/ppermute | solution.py:21
  104.4 15.1 %collective-permute-start.23 = (bf16[2,4,64,1280]{3,2,1,0:T(8,128)(2,1)}, bf16[2,4,64,1280]{3,2,1,0:T(8,128)(2,1)}, u32[]{:S(2)}, u32[]{:S(2)}) collective-permute-start(bf16[2,4,64,1280]{3,2,1,0:T(8,128)(2,1)} %collective-permute-done.16.refs_2_), channel_id=1, source_target_pairs={{0,1},{1,0},{2,3},{3,2},{4,5},{5,4},{6,7},{7,6},{8,9},{9,8},{10,11... | collective-permute-start | bytes 3932168 | tf_op jit(solution)/shard_map/ppermute | solution.py:21
  104.4 15.1 %collective-permute-start.24 = (bf16[2,4,64,1280]{3,2,1,0:T(8,128)(2,1)}, bf16[2,4,64,1280]{3,2,1,0:T(8,128)(2,1)}, u32[]{:S(2)}, u32[]{:S(2)}) collective-permute-start(bf16[2,4,64,1280]{3,2,1,0:T(8,128)(2,1)} %collective-permute-done.18.refs_3_), channel_id=1, source_target_pairs={{0,1},{1,0},{2,3},{3,2},{4,5},{5,4},{6,7},{7,6},{8,9},{9,8},{10,11... | collective-permute-start | bytes 3932168 | tf_op jit(solution)/shard_map/ppermute | solution.py:21
  105.3 0.8 copy-start.1
  129.6 17.3 %copy-start.9 = (s32[2,32]{1,0:T(2,128)S(1)}, s32[2,32]{1,0:T(2,128)}, u32[]{:S(2)}) copy-start(s32[2,32]{1,0:T(2,128)} %param.14) | copy-start | bytes 772
  129.6 17.3 %copy-start.10 = (f32[2,32]{1,0:T(2,128)S(1)}, f32[2,32]{1,0:T(2,128)}, u32[]{:S(2)}) copy-start(f32[2,32]{1,0:T(2,128)} %param.16) | copy-start | bytes 772
  130.5 15.9 %all-to-all-start.1 = ((f32[128,1,256]{2,1,0:T(1,128)}), f32[128,1,256]{2,1,0:T(1,128)S(1)}, u32[]{:S(2)}, u32[]{:S(2)}) async-start(f32[128,1,256]{2,1,0:T(1,128)} %copy.68), calls=%async_computation.1 | async-start | bytes 262144 | tf_op jit(solution)/shard_map/all_to_all | solution.py:336
  148.4 11.0 %all-to-all-start.2 = ((f32[16,1,2]{2,1,0:T(1,128)}), f32[16,1,2]{2,1,0:T(1,128)S(1)}, u32[]{:S(2)}, u32[]{:S(2)}) async-start(f32[16,1,2]{2,1,0:T(1,128)} %broadcast_in_dim.139), calls=%async_computation.2 | async-start | bytes 16384 | tf_op jit(solution)/shard_map/all_to_all | solution.py:350
